TPU v7x, 512 devices: a whole 4x8x8 slice. The times are simulated.
512 devices in a mesh: dp: 32 (over y_hi, x, core), axial: 16 (over z, y_lo).
Axes of the slice: x: 4, y: 8 (y_hi: 4, y_lo: 2; y = y_hi * 2 + y_lo), z: 8, core: 2. Of those that a mesh axis runs over, the one named last changes fastest.
Arguments:
- normed_homolog_features: bfloat16 [32, 128, 128, 256], P('dp', None, 'axial'), may hold values from -6 to 6
- first_factor_matrix: bfloat16 [256, 32], replicated, may hold values from -0.375 to 0.375
- second_factor_matrix: bfloat16 [256, 32], replicated, may hold values from -0.375 to 0.375
- output_weight: bfloat16 [1024, 128], replicated, may hold values from -2 to 2
- pair_update_gradient: float32 [32, 128, 128, 128], P('dp', 'axial'), may hold values from -6 to 6
Outputs:
- pair_update: float32 [32, 128, 128, 128], P('dp', 'axial')
- grad_msa: bfloat16 [32, 128, 128, 256], P('dp', None, 'axial')
- grad_left: float32 [256, 32], replicated
- grad_right: float32 [256, 32], replicated
- grad_out: float32 [1024, 128], replicated
All inputs are finite; a program needn't handle non-finite values.
Results may differ from a plain program's by a relative error of at most 0.007.
Values may be sent and summed in bfloat16 or wider, within the bound.
No kernel may reach another device: no remote copies, remote signals or barrier semaphores. Data moves between devices by JAX's collectives and lax.ppermute only.
A program may use at most 64 MiB of HBM per device.

v0:
```python
import jax
import jax.numpy as jnp
from jax import lax
from jax.sharding import PartitionSpec as P


def per_device(
    normed_homolog_features,
    first_factor_matrix,
    second_factor_matrix,
    output_weight,
    pair_update_gradient,
):
    example_homolog_entries = normed_homolog_features[0]
    alignment_depth, device_residues, alignment_width = example_homolog_entries.shape
    projected_width = first_factor_matrix.shape[1]
    cotangent = pair_update_gradient[0].astype(jnp.bfloat16)
    total_res = cotangent.shape[1]
    pair_width = cotangent.shape[2]
    homolog_matrix_merged = example_homolog_entries.reshape(
        alignment_depth * device_residues, alignment_width
    )
    left_projected = (
        jnp.dot(homolog_matrix_merged, first_factor_matrix, preferred_element_type=jnp.float32)
        .astype(jnp.bfloat16)
        .reshape(alignment_depth, device_residues, projected_width)
    )
    right_flat = (
        jnp.dot(homolog_matrix_merged, second_factor_matrix, preferred_element_type=jnp.float32)
        .astype(jnp.bfloat16)
        .reshape(alignment_depth, device_residues * projected_width)
    )
    device_block = lax.all_gather(right_flat, "axial", axis=1, tiled=True)
    right_full = jnp.zeros((1, 1), jnp.float32)
    residues_per_block = device_block.shape[1] // projected_width
    right_residue_block = device_block.reshape(alignment_depth, residues_per_block, projected_width)
    outer_flat = (
        (
            jnp.einsum(
                "sic,sje->ijce",
                left_projected,
                right_residue_block,
                preferred_element_type=jnp.float32,
            )
            / alignment_depth
        )
        .astype(jnp.bfloat16)
        .reshape(device_residues * residues_per_block, projected_width * projected_width)
    )
    grad_cols = cotangent.reshape(device_residues * residues_per_block, pair_width)
    update_block = jnp.dot(outer_flat, output_weight, preferred_element_type=jnp.float32).reshape(
        device_residues, residues_per_block, pair_width
    )
    pair_out = update_block
    output_weight_gradient = jnp.dot(outer_flat.T, grad_cols, preferred_element_type=jnp.float32)
    grad_outer = (
        jnp.dot(grad_cols, output_weight.T, preferred_element_type=jnp.float32)
        .astype(jnp.bfloat16)
        .reshape(device_residues, residues_per_block, projected_width, projected_width)
    )
    left_running_total = (
        jnp.einsum(
            "ijce,sje->sic", grad_outer, right_residue_block, preferred_element_type=jnp.float32
        )
        / alignment_depth
    )
    pair_out, output_weight_gradient, left_running_total, right_full = (
        pair_out,
        output_weight_gradient,
        left_running_total,
        right_full,
    )
    cot_columns = lax.all_to_all(cotangent, "axial", split_axis=1, concat_axis=0, tiled=True)
    left_flattened_rows = left_projected.reshape(alignment_depth, device_residues * projected_width)
    device_block = lax.all_gather(left_flattened_rows, "axial", axis=1, tiled=True)
    residues_per_block = device_block.shape[1] // projected_width
    left_residue_block = device_block.reshape(alignment_depth, residues_per_block, projected_width)
    grad_rows = cot_columns.reshape(residues_per_block * device_residues, pair_width)
    grad_outer = (
        jnp.dot(grad_rows, output_weight.T, preferred_element_type=jnp.float32)
        .astype(jnp.bfloat16)
        .reshape(residues_per_block, device_residues, projected_width, projected_width)
    )
    right_row_sum = (
        jnp.einsum(
            "ijce,sic->sje", grad_outer, left_residue_block, preferred_element_type=jnp.float32
        )
        / alignment_depth
    )
    first_factor_cotangent = left_running_total.astype(jnp.bfloat16).reshape(
        alignment_depth * device_residues, projected_width
    )
    second_factor_cotangent = right_row_sum.astype(jnp.bfloat16).reshape(
        alignment_depth * device_residues, projected_width
    )
    homolog_cotangent_entries = (
        jnp.dot(first_factor_cotangent, first_factor_matrix.T, preferred_element_type=jnp.float32)
        + jnp.dot(
            second_factor_cotangent, second_factor_matrix.T, preferred_element_type=jnp.float32
        )
    ).astype(jnp.bfloat16)
    left_weight_gradient = jnp.dot(
        homolog_matrix_merged.T, first_factor_cotangent, preferred_element_type=jnp.float32
    )
    right_weight_gradient = jnp.dot(
        homolog_matrix_merged.T, second_factor_cotangent, preferred_element_type=jnp.float32
    )
    left_weight_gradient, right_weight_gradient, output_weight_gradient = lax.psum(
        (left_weight_gradient, right_weight_gradient, output_weight_gradient), ("dp", "axial")
    )
    crop_count = lax.axis_size("dp")
    return (
        pair_out.reshape(1, device_residues, total_res, pair_width),
        homolog_cotangent_entries.reshape(1, alignment_depth, device_residues, alignment_width),
        left_weight_gradient / crop_count,
        right_weight_gradient / crop_count,
        output_weight_gradient / crop_count,
    )


def solution(mesh):
    in_specs = (P("dp", None, "axial", None), P(), P(), P(), P("dp", "axial", None, None))
    out_specs = (P("dp", "axial", None, None), P("dp", None, "axial", None), P(), P(), P())
    return jax.shard_map(
        per_device, mesh=mesh, in_specs=in_specs, out_specs=out_specs, check_vma=False
    )
```

profile of v0, /device:TPU:1, one launch (start us, length us, event | category | flops | bytes accessed | tf_op | source)
XLA Modules:
  0.0 705.5 jit_solution(17855057032200236086)
XLA Ops:
  7.2 1.0 copy-done
  8.2 1.0 convolution_convert_fusion.3
  10.3 1.1 convert_bitcast_fusion
  11.4 0.9 copy.76
  12.2 12.0 %all-to-all-start = ((bf16[8,128,128]{2,0,1:T(8,128)(2,1)}), bf16[8,128,128]{2,0,1:T(8,128)(2,1)}, u32[]{:S(2)}, u32[]{:S(2)}) async-start(bf16[8,128,128]{2,0,1:T(8,128)(2,1)} %copy.76), calls=%async_computation | async-start | bytes 524288 | tf_op jit(solution)/shard_map/all_to_all | solution.py:73
  26.5 8.0 %reshape.75 = bf16[8,128,32,32]{3,2,1,0:T(8,128)(2,1)} reshape(bf16[1024,1024]{1,0:T(8,128)(2,1)S(1)} %convolution_convert_fusion.1) | data formatting | bytes 4194304 | tf_op jit(solution)/shard_map/reshape | solution.py:59
  34.6 1.0 copy.78
  36.4 8.0 %reshape.64 = bf16[128,8,32,32]{3,2,1,0:T(8,128)(2,1)} reshape(bf16[1024,1024]{1,0:T(8,128)(2,1)S(1)} %convolution_convert_fusion) | data formatting | bytes 4194304 | tf_op jit(solution)/shard_map/reshape | solution.py:82
  44.3 32.1 %all-gather.3.cloned.1.call-done = bf16[128,4096]{1,0:T(8,128)(2,1)} async-done(((bf16[128,256]{1,0:T(8,128)(2,1)}), bf16[128,4096]{1,0:T(8,128)(2,1)}) %all-gather.3.cloned.1.call-update) | async-done | bytes 1048592 | tf_op jit(solution)/shard_map/all_gather | solution.py:33
  76.4 1.6 copy.65
  78.8 2.1 copy.81
  81.0 2.7 copy.69
  83.7 5.7 fusion.8
  90.4 1.3 fusion.18
  91.7 57.0 %all-gather.5.cloned.1.call-done = bf16[128,4096]{1,0:T(8,128)(2,1)} async-done(((bf16[128,256]{1,0:T(8,128)(2,1)}), bf16[128,4096]{1,0:T(8,128)(2,1)}) %all-gather.5.cloned.1.call-update) | async-done | bytes 1048592 | tf_op jit(solution)/shard_map/all_gather | solution.py:75
  148.7 1.6 copy.75
  150.3 5.7 fusion.9
  157.1 3.1 fusion
  160.3 1.5 convolution_bitcast_fusion
  161.9 2.3 fusion.5
  164.1 265.4 %all-reduce.6.cloned.1.call-done = (f32[256,32]{0,1:T(8,128)}, f32[256,32]{0,1:T(8,128)}) async-done(((f32[256,32]{0,1:T(8,128)}, f32[256,32]{0,1:T(8,128)}), (f32[256,32]{0,1:T(8,128)}, f32[256,32]{0,1:T(8,128)})) %all-reduce.6.cloned.1.call-update) | async-done | bytes 65552 | tf_op jit(solution)/shard_map/psum | solution.py:108
  429.6 1.4 broadcast_multiply_fusion.1
  431.0 266.1 %all-reduce.4.cloned.1.call-done = f32[1024,128]{1,0:T(8,128)} async-done(((f32[1024,128]{1,0:T(8,128)}), f32[1024,128]{1,0:T(8,128)}) %all-reduce.4.cloned.1.call-update) | async-done | bytes 524304 | tf_op jit(solution)/shard_map/psum | solution.py:108
  697.1 1.9 broadcast_multiply_fusion
  (34 shorter events, 7.1 us)
Async XLA Ops:
  7.2 1.1 copy-start
  7.2 18.5 %copy-start.3 = (f32[1,8,128,128]{3,2,1,0:T(8,128)S(1)}, f32[1,8,128,128]{3,2,1,0:T(8,128)}, u32[]{:S(2)}) copy-start(f32[1,8,128,128]{3,2,1,0:T(8,128)} %param.9) | copy-start | bytes 1572868
  7.2 17.1 %copy-start.5 = (bf16[256,32]{0,1:T(8,128)(2,1)S(1)}, bf16[256,32]{0,1:T(8,128)(2,1)}, u32[]{:S(2)}) copy-start(bf16[256,32]{0,1:T(8,128)(2,1)} %param.6) | copy-start | bytes 49156
  7.2 69.2 %all-gather.3.cloned.1.call-start = ((), (), s32[]{:S(2)}) async-start(), calls=%async_computation.1 | async-start | bytes 1114112 | tf_op jit(solution)/shard_map/all_gather | solution.py:33
  9.4 16.4 %copy-start.2 = (bf16[1024,128]{1,0:T(8,128)(2,1)S(1)}, bf16[1024,128]{1,0:T(8,128)(2,1)}, u32[]{:S(2)}) copy-start(bf16[1024,128]{1,0:T(8,128)(2,1)} %param.8) | copy-start | bytes 786436
  12.2 22.4 %all-to-all-start = ((bf16[8,128,128]{2,0,1:T(8,128)(2,1)}), bf16[8,128,128]{2,0,1:T(8,128)(2,1)}, u32[]{:S(2)}, u32[]{:S(2)}) async-start(bf16[8,128,128]{2,0,1:T(8,128)(2,1)} %copy.76), calls=%async_computation | async-start | bytes 524288 | tf_op jit(solution)/shard_map/all_to_all | solution.py:73
  24.3 124.4 %all-gather.5.cloned.1.call-start = ((), (), s32[]{:S(2)}) async-start(), calls=%async_computation.2 | async-start | bytes 1114112 | tf_op jit(solution)/shard_map/all_gather | solution.py:75
  25.6 403.9 %all-reduce.6.cloned.1.call-start = ((), (), s32[]{:S(2)}) async-start(), calls=%async_computation.4 | async-start | bytes 131072 | tf_op jit(solution)/shard_map/psum | solution.py:108
  156.2 4.0 copy-start.1
  160.2 1.7 copy-start.4
  160.2 536.9 %all-reduce.4.cloned.1.call-start = ((), (), s32[]{:S(2)}) async-start(), calls=%async_computation.3 | async-start | bytes 1048576 | tf_op jit(solution)/shard_map/psum | solution.py:108
Sparse Core Ops, SparseCore 0:
  10.6 65.7 all-gather.2
  79.0 69.6 all-gather.4
  160.3 269.2 all-reduce.5
  435.8 261.2 all-reduce.3
where the time goes:
time: 706 us
  waiting for transfers between devices  621 us (88%)
  local copies, waits for them, and re-layouts  29.5 us (4%)
  matrix products  24.7 us (3%)
  between operations  14 us (2%)
  starting transfers between devices  12.2 us (2%)
    psum x2, waiting for transfers between devices, per_device(): lax.psum((left_weight_gradient, right_weight_gradient, output_weight_grad...  532 us
    all_gather x1, waiting for transfers between devices, per_device(): lax.all_gather(left_flattened_rows, 'axial', axis=1, tiled=True)  57 us
    all_gather x1, waiting for transfers between devices, per_device(): device_block = lax.all_gather(right_flat, 'axial', axis=1, tiled=True)  32.1 us
  transfers between devices with their start and end apart: 5, of which 4 were waited for; matrix products, arithmetic and copies ran while one was open for 6% of the time, Pallas kernels for 0%

commit v1 on v0

v1 whole, which is shorter than its diff:
```python
import jax
import jax.numpy as jnp
from jax import lax
from jax.experimental import pallas as pl
from jax.experimental.pallas import tpu as pltpu
from jax.sharding import Mesh, PartitionSpec as P

BF16 = jnp.bfloat16
F32 = jnp.float32
ROW = ("zl", "yl")
COL = "zh"
XC = ("x", "core")
YH = "yh"
AXIAL = ("zh", "zl", "yl")
DP = ("yh", "x", "core")

S = 128
RES = 8
C = 32
Z = 128
F = 256
G = 4


def dot(a, b, dims):
    return lax.dot_general(a, b, (dims, ((), ())), preferred_element_type=F32)


def nn(a, b):
    return dot(a, b, ((1,), (0,)))


def nt(a, b):
    return dot(a, b, ((1,), (1,)))


def tn(a, b):
    return dot(a, b, ((0,), (0,)))


def call(kernel, out, *args, scratch=(), flops=0):
    size = sum(a.size * a.dtype.itemsize for a in args) + sum(
        o.size * o.dtype.itemsize for o in out
    )
    return pl.pallas_call(
        kernel,
        out_shape=out,
        in_specs=[pl.BlockSpec(memory_space=pltpu.VMEM)] * len(args),
        out_specs=[pl.BlockSpec(memory_space=pltpu.VMEM)] * len(out),
        scratch_shapes=list(scratch),
        compiler_params=pltpu.CompilerParams(vmem_limit_bytes=48 * 1024 * 1024),
        cost_estimate=pl.CostEstimate(flops=flops, bytes_accessed=size, transcendentals=0),
    )(*args)


def shape(dims, dtype):
    return jax.ShapeDtypeStruct(dims, dtype)


def exchange(x, axes):
    return lax.all_to_all(x, axes, split_axis=0, concat_axis=0, tiled=True)


def channel_major():
    n = RES * C
    p = lax.broadcasted_iota(jnp.int32, (n, n), 0)
    q = lax.broadcasted_iota(jnp.int32, (n, n), 1)
    same = ((p >> 3) == (q & 31)) & ((p & 7) == (q >> 5))
    return jnp.where(same, 1.0, 0.0).astype(BF16)


def project_kernel(x_ref, f1_ref, f2_ref, cot_ref, row_ref, col_ref):
    for b in range(G):
        for i in range(RES):
            for h in range(2):
                at = i * 128 + h * 64 + b * 8
                pair = jnp.concatenate([cot_ref[at : at + 8, :], cot_ref[at + 32 : at + 40, :]], axis=0)
                row_ref[b, i * 32 + h * 16 : i * 32 + h * 16 + 16, :] = pair.astype(BF16)
    factors = jnp.concatenate([f1_ref[...].astype(F32).T, f2_ref[...].astype(F32).T], axis=0).astype(BF16)
    left, right = [], []
    for i in range(RES):
        both = nt(factors, x_ref[i]).astype(BF16)
        left.append(both[:C])
        right.append(both[C:])
    left = jnp.concatenate(left, axis=0)
    right = nn(channel_major(), jnp.concatenate(right, axis=0)).astype(BF16)
    for b in range(G):
        row_ref[b, 256:512, :] = left
        col_ref[b] = right


def swap_to_channels(o):
    blocks = []
    for e in range(C):
        at = e * 32
        blocks.append(
            jnp.concatenate([o[i * 32 : i * 32 + 32, at : at + 32] for i in range(4)], axis=1)
        )
    return jnp.concatenate(blocks, axis=0)


def swap_to_residues(g):
    rows = []
    for i in range(4):
        rows.append(
            jnp.concatenate(
                [g[e * 32 : e * 32 + 32, i * 32 : i * 32 + 32] for e in range(C)], axis=1
            )
        )
    return jnp.concatenate(rows, axis=0)


def main_kernel(row_ref, col_ref, w_ref, out_ref, rg_ref, wide, gout, grads):
    wide[...] = w_ref[...].astype(F32)
    weight = jnp.concatenate([wide[pl.ds(e, 32, stride=32), :] for e in range(C)], axis=0)
    weight_t = weight.T.astype(BF16)
    weight = weight.astype(BF16)
    right = jnp.concatenate(
        [col_ref[a].astype(F32).reshape(C, RES, S) for a in range(G)], axis=1
    ).reshape(C * G * RES, S).astype(BF16)
    for q in range(8):
        b, at = q // 2, (q % 2) * 128
        left = row_ref[b, 256 + at : 256 + at + 128, :]
        cot = row_ref[b, at : at + 128, :]
        outer = swap_to_channels((nt(left, right) * (1.0 / S)).astype(BF16))
        out_ref[b, at : at + 128, :] = nn(weight_t, outer).T.astype(BF16)
        term = nn(outer, cot)
        if q == 0:
            gout[...] = term
        else:
            gout[...] += term
        grad = swap_to_residues(nt(weight, cot).astype(BF16))
        grads[q * 128 : q * 128 + 128, :] = grad
        out_ref[b, 256 + at : 256 + at + 128, :] = (nn(grad, right) * (1.0 / S)).astype(BF16)
    for b in range(G):
        out_ref[b, 512:768, :] = gout[b * 256 : b * 256 + 256, :].astype(BF16)
    lefts = jnp.concatenate([row_ref[b, 256:512, :] for b in range(G)], axis=0)
    rg = (tn(lefts, grads[...]) * (1.0 / S)).T.reshape(C, G, RES, S)
    for a in range(G):
        rg_ref[a] = rg[:, a].reshape(C * RES, S).astype(BF16)


def merge_kernel(back_ref, rg_ref, col_ref):
    total = sum(back_ref[b, 512:768, :].astype(F32) for b in range(G)).astype(BF16)
    for a in range(G):
        col_ref[a, 0:256, :] = rg_ref[a]
        col_ref[a, 256:320, :] = total[a * 64 : a * 64 + 64]


def update_kernel(back_ref, out_ref):
    for b in range(G):
        part = back_ref[b, 0:256, :].astype(F32)
        for i in range(RES):
            for a in range(G):
                at = i * 128 + a * 32 + b * 8
                out_ref[at : at + 8, :] = part[i * 32 + a * 8 : i * 32 + a * 8 + 8, :]


def factor_kernel(back_ref, col_ref, x_ref, grad_ref, tail_ref):
    left = sum(back_ref[b, 256:512, :].astype(F32) for b in range(G)).astype(BF16)
    right = sum(col_ref[a, 0:256, :].astype(F32) for a in range(G)).astype(BF16)
    right = tn(channel_major(), right).astype(BF16)
    total = jnp.zeros((2 * C, F), F32)
    for i in range(RES):
        both = jnp.concatenate([left[i * C : i * C + C], right[i * C : i * C + C]], axis=0)
        grad_ref[i] = both
        total = total + nn(both, x_ref[i])
    gout = sum(col_ref[a, 256:320, :].astype(F32) for a in range(G))
    for k in range(8):
        half, at = k // 4, (k % 4) * 16
        tail_ref[k, 0:16, :] = total[at : at + 16, half * 128 : half * 128 + 128]
        tail_ref[k, 16:24, :] = gout[k * 8 : k * 8 + 8]


def msa_kernel(grad_ref, f1_ref, f2_ref, out_ref):
    factors = jnp.concatenate([f1_ref[...].astype(F32).T, f2_ref[...].astype(F32).T], axis=0).astype(BF16)
    for i in range(RES):
        out_ref[i] = tn(grad_ref[i], factors).astype(BF16)


def sum_kernel(in_ref, out_ref):
    total = in_ref[0]
    for k in range(1, in_ref.shape[0]):
        total = total + in_ref[k]
    for k in range(out_ref.shape[0]):
        out_ref[k] = total


def gather_kernel(in_ref, out_ref):
    total = in_ref[0, 0:16, :]
    for k in range(1, 16):
        total = total + in_ref[k, 0:16, :]
    total = total.astype(BF16)
    gout = jnp.concatenate([in_ref[k, 16:24, :] for k in range(16)], axis=0).astype(BF16)
    for k in range(8):
        out_ref[k, 0:16, :] = total
        out_ref[k, 16:144, :] = gout


def final_kernel(in_ref, gl_ref, gr_ref, gout_ref, wide):
    scale = 1.0 / 32
    halves = [
        jnp.concatenate([in_ref[h * 4 + k, 0:16, :].astype(F32) for k in range(4)], axis=0)
        for h in range(2)
    ]
    both = jnp.concatenate(halves, axis=1).T * scale
    gl_ref[...] = both[:, 0:C]
    gr_ref[...] = both[:, C : 2 * C]
    for k in range(8):
        part = in_ref[k, 16:144, :].astype(F32) * scale
        for a in range(G):
            for b in range(G):
                at = b * 256 + a * 64 + k * 8
                wide[at : at + 8, :] = part[(a * 4 + b) * 8 : (a * 4 + b) * 8 + 8]
    for c in range(C):
        gout_ref[c * 32 : c * 32 + 32, :] = wide[pl.ds(c, 32, stride=32), :]


def per_device(x, f1, f2, w, cot):
    x = x[0].transpose(1, 0, 2)
    cot = cot[0].reshape(RES * 128, Z)
    row, col = call(
        project_kernel, [shape((G, 512, S), BF16), shape((G, 256, S), BF16)], x, f1, f2, cot, flops=33554432
    )
    row = exchange(row, ROW)
    col = exchange(col, COL)
    back, rg = call(
        main_kernel,
        [shape((G, 768, 128), BF16), shape((G, 256, S), BF16)],
        row,
        col,
        w,
        scratch=[pltpu.VMEM((1024, 128), F32), pltpu.VMEM((1024, 128), F32), pltpu.VMEM((1024, 1024), BF16)],
        flops=6 * 2 * 1024 * 1024 * 128,
    )
    back = exchange(back, ROW)
    (col,) = call(merge_kernel, [shape((G, 320, 128), BF16)], back, rg)
    col = exchange(col, COL)
    (update,) = call(update_kernel, [shape((RES * 128, Z), F32)], back)
    grad, tail = call(
        factor_kernel, [shape((RES, 2 * C, S), BF16), shape((8, 24, 128), F32)], back, col, x, flops=33554432
    )
    (msa,) = call(msa_kernel, [shape((RES, S, F), BF16)], grad, f1, f2, flops=33554432)
    tail = exchange(tail, XC)
    (tail,) = call(sum_kernel, [shape((G, 24, 128), F32)], tail)
    tail = exchange(tail, YH)
    (tail,) = call(sum_kernel, [shape((16, 24, 128), F32)], tail)
    tail = exchange(tail, AXIAL)
    (tail,) = call(gather_kernel, [shape((8, 144, 128), BF16)], tail)
    tail = exchange(tail, XC)
    gl, gr, gout = call(
        final_kernel,
        [shape((F, C), F32), shape((F, C), F32), shape((1024, 128), F32)],
        tail,
        scratch=[pltpu.VMEM((1024, 128), F32)],
    )
    return update.reshape(1, RES, 128, Z), msa.transpose(1, 0, 2)[None], gl, gr, gout


def solution(mesh):
    split = Mesh(mesh.devices.reshape(4, 4, 2, 4, 2, 2), ("yh", "x", "core", "zh", "zl", "yl"))
    in_specs = (P(DP, None, AXIAL, None), P(), P(), P(), P(DP, AXIAL, None, None))
    out_specs = (P(DP, AXIAL, None, None), P(DP, None, AXIAL, None), P(), P(), P())
    return jax.shard_map(per_device, mesh=split, in_specs=in_specs, out_specs=out_specs, check_vma=False)
```

time: 706 us -> 120 us (0.17)
  waiting for transfers between devices: 621 us -> 4.51 us
  blocking collectives: 0 us -> 92 us
  local copies, waits for them, and re-layouts: 29.5 us -> 4.64 us
  matrix products: 24.7 us -> 0 us
  between operations: 14 us -> 0.72 us
  Pallas kernels: 0 us -> 11.1 us
    psum x2 -> x0, waiting for transfers between devices: 532 us -> none  [per_device(): lax.psum((left_weight_gradient, right_weight_gradient, output_weight_grad...]
    all_to_all x0 -> x7, blocking collectives: none -> 92 us  [exchange(): return lax.all_to_all(x, axes, split_axis=0, concat_axis=0, tiled=True)]
    all_gather x2 -> x0, waiting for transfers between devices: 89.1 us -> none  [the longest x1 57 us: per_device(): lax.all_gather(left_flattened_rows, 'axial', axis=1, tiled=True)]
    dot_general x13 -> x0, matrix products: 24.7 us -> none  [the longest x1 5.71 us: per_device(): jnp.einsum('ijce,sic->sje', grad_outer, left_residue_block, preferred_ele...]
    reshape x4 -> x0, local copies, waits for them, and re-layouts: 17 us -> none  [the longest x1 7.97 us: per_device(): grad_outer = jnp.dot(grad_rows, output_weight.T, preferred_element_type=j...]
    pallas_call x0 -> x10, Pallas kernels: none -> 11.1 us  [call(): pl.pallas_call(kernel, out_shape=out, in_specs=[pl.BlockSpec(memory_space...]
  transfers between devices with their start and end apart: 5 -> 1, of which waited for: 4 -> 1; matrix products, arithmetic and copies ran while one was open for 6% -> 1% of each run, Pallas kernels for 0% -> 1%
where the time goes in v1:
time: 120 us
  blocking collectives  92 us (77%)
  Pallas kernels  11.1 us (9%)
  starting transfers between devices  6.85 us (6%)
  local copies, waits for them, and re-layouts  4.64 us (4%)
  waiting for transfers between devices  4.51 us (4%)
    all_to_all x7, blocking collectives, exchange(): return lax.all_to_all(x, axes, split_axis=0, concat_axis=0, tiled=True)  92 us
    pallas_call x10, Pallas kernels, call(): pl.pallas_call(kernel, out_shape=out, in_specs=[pl.BlockSpec(memory_space...  11.1 us
    all_to_all x1, starting transfers between devices, exchange(): return lax.all_to_all(x, axes, split_axis=0, concat_axis=0, tiled=True)  6.85 us
    unnamed x12, local copies, waits for them, and re-layouts  4.64 us
    all_to_all x1, waiting for transfers between devices, exchange(): return lax.all_to_all(x, axes, split_axis=0, concat_axis=0, tiled=True)  4.51 us
  transfers between devices with their start and end apart: 1, of which 1 were waited for; matrix products, arithmetic and copies ran while one was open for 1% of the time, Pallas kernels for 1%

profile of v1, /device:TPU:1, one launch (start us, length us, event | category | flops | bytes accessed | tf_op | source)
XLA Modules:
  0.0 119.8 jit_solution(7073275027711476072)
XLA Ops:
  0.6 0.8 copy.11.f1_ref
  1.5 0.0 copy-done.2
  1.5 0.1 copy.12.f2_ref
  1.6 0.0 copy-start
  1.6 1.2 %copy.19 = bf16[1,128,8,256]{3,1,2,0:T(8,128)(2,1)S(1)} copy(bf16[1,128,8,256]{3,2,1,0:T(8,128)(2,1)} %param.5) | data formatting | bytes 1048576 | tf_op args[0]
  2.8 0.6 shard_map.92
  3.4 19.4 %all_to_all.40.col_ref = bf16[4,256,128]{2,1,0:T(8,128)(2,1)S(1)} all-to-all(bf16[4,256,128]{2,1,0:T(8,128)(2,1)S(1)} %get-tuple-element.15), channel_id=1, replica_groups=mesh['yh'=4,'x'=4,'core'=2,'zh'=4,'zl'=2,'yl'=2] {'zh'}, dimensions={0} | all-to-all | bytes 524288 | tf_op jit(solution)/shard_map/all_to_all | solution.py:61
  22.8 10.9 %all_to_all.41.row_ref = bf16[4,512,128]{2,1,0:T(8,128)(2,1)S(1)} all-to-all(bf16[4,512,128]{2,1,0:T(8,128)(2,1)S(1)} %get-tuple-element.14), channel_id=1, replica_groups=mesh['yh'=4,'x'=4,'core'=2,'zh'=4,'zl'=2,'yl'=2] {'zl','yl'}, dimensions={0} | all-to-all | bytes 1048576 | tf_op jit(solution)/shard_map/all_to_all | solution.py:61
  33.6 6.8 %shard_map.93 = (bf16[4,768,128]{2,1,0:T(8,128)(2,1)S(1)}, bf16[4,256,128]{2,1,0:T(8,128)(2,1)S(1)}) custom-call(bf16[4,512,128]{2,1,0:T(8,128)(2,1)S(1)} %all_to_all.41.row_ref, bf16[4,256,128]{2,1,0:T(8,128)(2,1)S(1)} %all_to_all.40.col_ref, bf16[1024,128]{1,0:T(8,128)(2,1)S(1)} %copy-done.1), custom_call_target="tpu_custom_call" | custom-call | flops 1610612736 | bytes 2097152 | tf_op jit(solution)/shard_map/pallas_call | solution.py:45
  40.5 9.8 %all_to_all.42.back_ref = bf16[4,768,128]{2,1,0:T(8,128)(2,1)S(1)} all-to-all(bf16[4,768,128]{2,1,0:T(8,128)(2,1)S(1)} %get-tuple-element.16), channel_id=1, replica_groups=mesh['yh'=4,'x'=4,'core'=2,'zh'=4,'zl'=2,'yl'=2] {'zl','yl'}, dimensions={0} | all-to-all | bytes 1572864 | tf_op jit(solution)/shard_map/all_to_all | solution.py:61
  50.4 13.2 %all_to_all.43.col_ref = bf16[4,320,128]{2,1,0:T(8,128)(2,1)S(1)} all-to-all(bf16[4,320,128]{2,1,0:T(8,128)(2,1)S(1)} %shard_map.95), channel_id=1, replica_groups=mesh['yh'=4,'x'=4,'core'=2,'zh'=4,'zl'=2,'yl'=2] {'zh'}, dimensions={0} | all-to-all | bytes 655360 | tf_op jit(solution)/shard_map/all_to_all | solution.py:61
  63.6 0.4 shard_map.96
  64.0 14.4 %all_to_all.44.in_ref = f32[8,24,128]{2,1,0:T(8,128)S(1)} all-to-all(f32[8,24,128]{2,1,0:T(8,128)S(1)} %get-tuple-element.19), channel_id=1, replica_groups=mesh['yh'=4,'x'=4,'core'=2,'zh'=4,'zl'=2,'yl'=2] {'x','core'}, dimensions={0} | all-to-all | bytes 196608 | tf_op jit(solution)/shard_map/all_to_all | solution.py:61
  78.5 12.8 %all_to_all.45.in_ref = f32[4,24,128]{2,1,0:T(8,128)S(1)} all-to-all(f32[4,24,128]{2,1,0:T(8,128)S(1)} %shard_map.98), channel_id=1, replica_groups=mesh['yh'=4,'x'=4,'core'=2,'zh'=4,'zl'=2,'yl'=2] {'yh'}, dimensions={0} | all-to-all | bytes 98304 | tf_op jit(solution)/shard_map/all_to_all | solution.py:61
  91.2 11.5 %all_to_all.46.in_ref = f32[16,24,128]{2,1,0:T(8,128)S(1)} all-to-all(f32[16,24,128]{2,1,0:T(8,128)S(1)} %shard_map.99), channel_id=1, replica_groups=mesh['yh'=4,'x'=4,'core'=2,'zh'=4,'zl'=2,'yl'=2] {'zh','zl','yl'}, dimensions={0} | all-to-all | bytes 393216 | tf_op jit(solution)/shard_map/all_to_all | solution.py:61
  102.7 0.7 shard_map.100
  103.5 6.9 %all-to-all-start.7 = ((bf16[8,144,128]{2,1,0:T(8,128)(2,1)}), bf16[8,144,128]{2,1,0:T(8,128)(2,1)S(1)}, u32[]{:S(2)}, u32[]{:S(2)}) async-start(bf16[8,144,128]{2,1,0:T(8,128)(2,1)} %shard_map.100), calls=%async_computation.7 | async-start | bytes 589824 | tf_op jit(solution)/shard_map/all_to_all | solution.py:61
  110.3 0.9 shard_map.94
  111.2 0.4 shard_map.97
  111.6 1.1 copy.15
  112.6 4.5 %all-to-all-done.7.in_ref = bf16[8,144,128]{2,1,0:T(8,128)(2,1)S(1)} async-done(((bf16[8,144,128]{2,1,0:T(8,128)(2,1)}), bf16[8,144,128]{2,1,0:T(8,128)(2,1)S(1)}, u32[]{:S(2)}, u32[]{:S(2)}) %all-to-all-start.7) | async-done | bytes 294944 | tf_op jit(solution)/shard_map/all_to_all | solution.py:61
  117.2 1.3 %shard_map.101 = (f32[256,32]{1,0:T(8,128)S(1)}, f32[256,32]{1,0:T(8,128)S(1)}, f32[1024,128]{1,0:T(8,128)}) custom-call(bf16[8,144,128]{2,1,0:T(8,128)(2,1)S(1)} %all-to-all-done.7.in_ref), custom_call_target="tpu_custom_call" | custom-call | bytes 884736 | tf_op jit(solution)/shard_map/pallas_call | solution.py:45
  118.4 0.7 copy.16
  119.1 0.7 copy.17
  (7 shorter events, 0.1 us)
Async XLA Ops:
  0.6 0.9 copy-start.2
  1.6 1.2 %copy-start = (f32[1,8,128,128]{3,2,1,0:T(8,128)S(1)}, f32[1,8,128,128]{3,2,1,0:T(8,128)}, u32[]{:S(2)}) copy-start(f32[1,8,128,128]{3,2,1,0:T(8,128)} %param.9) | copy-start | bytes 1572868
  22.8 10.9 %copy-start.1 = (bf16[1024,128]{1,0:T(8,128)(2,1)S(1)}, bf16[1024,128]{1,0:T(8,128)(2,1)}, u32[]{:S(2)}) copy-start(bf16[1024,128]{1,0:T(8,128)(2,1)} %w_ref.1) | copy-start | bytes 786436
  103.5 13.7 %all-to-all-start.7 = ((bf16[8,144,128]{2,1,0:T(8,128)(2,1)}), bf16[8,144,128]{2,1,0:T(8,128)(2,1)S(1)}, u32[]{:S(2)}, u32[]{:S(2)}) async-start(bf16[8,144,128]{2,1,0:T(8,128)(2,1)} %shard_map.100), calls=%async_computation.7 | async-start | bytes 589824 | tf_op jit(solution)/shard_map/all_to_all | solution.py:61

commit v2 on v1

v2 whole, which is shorter than its diff:
```python
import jax
import jax.numpy as jnp
from jax import lax
from jax.experimental import pallas as pl
from jax.experimental.pallas import tpu as pltpu
from jax.sharding import Mesh, PartitionSpec as P

BF16 = jnp.bfloat16
F32 = jnp.float32
ROW = ("zl", "yl")
COL = "zh"
NEAR = ("x", "core", "zl", "yl")
FAR = ("yh", "zh")
AXIAL = ("zh", "zl", "yl")
DP = ("yh", "x", "core")

S = 128
RES = 8
C = 32
Z = 128
F = 256
G = 4


def dot(a, b, dims):
    return lax.dot_general(a, b, (dims, ((), ())), preferred_element_type=F32)


def nn(a, b):
    return dot(a, b, ((1,), (0,)))


def nt(a, b):
    return dot(a, b, ((1,), (1,)))


def tn(a, b):
    return dot(a, b, ((0,), (0,)))


def call(kernel, out, *args, scratch=(), flops=0, hbm=False, limit=96):
    size = sum(a.size * a.dtype.itemsize for a in args) + sum(
        o.size * o.dtype.itemsize for o in out
    )
    return pl.pallas_call(
        kernel,
        out_shape=out,
        in_specs=[pl.BlockSpec(memory_space=pltpu.HBM if hbm else pltpu.VMEM)] * len(args),
        out_specs=[pl.BlockSpec(memory_space=pltpu.VMEM)] * len(out),
        scratch_shapes=list(scratch),
        compiler_params=pltpu.CompilerParams(vmem_limit_bytes=limit * 1024 * 256),
        cost_estimate=pl.CostEstimate(flops=flops, bytes_accessed=size, transcendentals=0),
    )(*args)


def shape(dims, dtype):
    return jax.ShapeDtypeStruct(dims, dtype)


def exchange(x, axes):
    return lax.all_to_all(x, axes, split_axis=0, concat_axis=0, tiled=True)


def channel_major():
    n = RES * C
    p = lax.broadcasted_iota(jnp.int32, (n, n), 0)
    q = lax.broadcasted_iota(jnp.int32, (n, n), 1)
    same = ((p >> 3) == (q & 31)) & ((p & 7) == (q >> 5))
    return jnp.where(same, 1.0, 0.0).astype(BF16)


def project_kernel(x_hbm, f_hbm, cot_hbm, row_ref, right_ref, xt_ref, x_ref, f_ref, cot_ref, wide, sems):
    copies = [
        pltpu.make_async_copy(f_hbm, f_ref, sems.at[0]),
        pltpu.make_async_copy(x_hbm, x_ref, sems.at[1]),
        pltpu.make_async_copy(cot_hbm, cot_ref, sems.at[2]),
    ]
    for copy in copies:
        copy.start()
    for copy in copies[:2]:
        copy.wait()
    factors = f_ref[...]
    for h in range(2):
        wide[h] = x_ref[:, h * 128 : h * 128 + 128].astype(F32)
    left, right = [], []
    for i in range(RES):
        x = jnp.concatenate([wide[h, pl.ds(i, S, stride=RES), :] for h in range(2)], axis=1).astype(BF16)
        xt_ref[i] = x
        both = nt(factors, x).astype(BF16)
        left.append(both[:C])
        right.append(both[C:])
    left = jnp.concatenate(left, axis=0)
    for b in range(G):
        row_ref[b, 256:512, :] = left
    right_ref[...] = nn(channel_major(), jnp.concatenate(right, axis=0)).astype(BF16)
    copies[2].wait()
    for b in range(G):
        for i in range(RES):
            for h in range(2):
                at = i * 128 + h * 64 + b * 8
                pair = jnp.concatenate([cot_ref[at : at + 8, :], cot_ref[at + 32 : at + 40, :]], axis=0)
                row_ref[b, i * 32 + h * 16 : i * 32 + h * 16 + 16, :] = pair.astype(BF16)


def swap_to_channels(o):
    n = o.shape[0] // C
    blocks = []
    for e in range(C):
        at = e * 32
        blocks.append(
            jnp.concatenate([o[i * 32 : i * 32 + 32, at : at + 32] for i in range(n)], axis=1)
        )
    return jnp.concatenate(blocks, axis=0)


def swap_to_residues(g):
    n = g.shape[1] // 32
    rows = []
    for i in range(n):
        rows.append(
            jnp.concatenate(
                [g[e * 32 : e * 32 + 32, i * 32 : i * 32 + 32] for e in range(C)], axis=1
            )
        )
    return jnp.concatenate(rows, axis=0)


def right_kernel(row_ref, right_ref, w_ref, col_ref, grads_ref, weight_ref, wide):
    wide[...] = w_ref[...].astype(F32)
    weight = jnp.concatenate([wide[pl.ds(e, 32, stride=32), :] for e in range(C)], axis=0)
    weight_ref[...] = weight.T.astype(BF16)
    weight = weight.astype(BF16)
    for b in range(G):
        grads_ref[b * 256 : b * 256 + 256, :] = swap_to_residues(
            nt(weight, row_ref[b, 0:256, :]).astype(BF16)
        )
    lefts = jnp.concatenate([row_ref[b, 256:512, :] for b in range(G)], axis=0)
    rg = (tn(lefts, grads_ref[...]) * (1.0 / S)).T.reshape(C, G, RES, S)
    for a in range(G):
        col_ref[a, 0:256, :] = rg[:, a].reshape(C * RES, S).astype(BF16)
        col_ref[a, 256:512, :] = right_ref[...]


def left_kernel(row_ref, col_ref, grads_ref, weight_ref, out_ref, gout_ref, outers):
    right = jnp.concatenate(
        [col_ref[a, 256:512, :].astype(F32).reshape(C, RES, S) for a in range(G)], axis=1
    ).reshape(C * G * RES, S).astype(BF16)
    for b in range(G):
        outer = swap_to_channels((nt(row_ref[b, 256:512, :], right) * (1.0 / S)).astype(BF16))
        outers[:, b * 256 : b * 256 + 256] = outer
        out_ref[b, 0:256, :] = nn(weight_ref[...], outer).T.astype(BF16)
        out_ref[b, 256:512, :] = (nn(grads_ref[b * 256 : b * 256 + 256, :], right) * (1.0 / S)).astype(BF16)
    cot = jnp.concatenate([row_ref[b, 0:256, :] for b in range(G)], axis=0)
    gout_ref[...] = nn(outers[...], cot).astype(BF16)


def right_factor_kernel(col_ref, x_ref, right_ref, gr_ref):
    right = sum(col_ref[a, 0:256, :].astype(F32) for a in range(G)).astype(BF16)
    right = tn(channel_major(), right).astype(BF16)
    right_ref[...] = right
    gr_ref[...] = sum(nn(right[i * C : i * C + C], x_ref[i]) for i in range(RES))


def left_factor_kernel(back_ref, gr_ref, x_ref, gout_ref, left_ref, tail_ref):
    left = sum(back_ref[b, 256:512, :].astype(F32) for b in range(G)).astype(BF16)
    left_ref[...] = left
    gl = sum(nn(left[i * C : i * C + C], x_ref[i]) for i in range(RES))
    total = jnp.concatenate([gl, gr_ref[...]], axis=0)
    rows = jnp.concatenate([total[:, 0:128], total[:, 128:256]], axis=0)
    pad = jnp.zeros((4, 128), F32)
    for k in range(C):
        tail_ref[k] = jnp.concatenate(
            [gout_ref[k * 32 : k * 32 + 32, :].astype(F32), rows[k * 4 : k * 4 + 4], pad], axis=0
        ).astype(BF16)


def update_kernel(back_ref, out_ref):
    for b in range(G):
        part = back_ref[b, 0:256, :].astype(F32)
        for i in range(RES):
            for a in range(G):
                at = i * 128 + a * 32 + b * 8
                out_ref[at : at + 8, :] = part[i * 32 + a * 8 : i * 32 + a * 8 + 8, :]


def msa_kernel(left_ref, right_ref, f_ref, out_ref):
    factors = f_ref[...]
    for i in range(RES):
        both = jnp.concatenate([left_ref[i * C : i * C + C, :], right_ref[i * C : i * C + C, :]], axis=0)
        out_ref[i] = tn(both, factors).astype(BF16)


def sum_kernel(in_ref, out_ref):
    total = in_ref[0].astype(F32)
    for k in range(1, in_ref.shape[0]):
        total = total + in_ref[k].astype(F32)
    total = total.astype(BF16)
    for k in range(out_ref.shape[0]):
        out_ref[k] = total


def final_kernel(in_ref, gl_ref, gr_ref, gout_ref, wide):
    scale = 1.0 / 32
    rows = []
    for e in range(C):
        part = in_ref[e].astype(F32) * scale
        wide[e * 32 : e * 32 + 32, :] = part[0:32]
        rows.append(part[32:36])
    for h in range(2):
        for q, out in enumerate((gl_ref, gr_ref)):
            at = h * 16 + q * 8
            out[:, h * 128 : h * 128 + 128] = jnp.concatenate(rows[at : at + 8], axis=0)
    for c in range(C):
        gout_ref[c * 32 : c * 32 + 32, :] = wide[pl.ds(c, 32, stride=32), :]


def per_device(x, f1, f2, w, cot):
    x = x[0].reshape(S * RES, F)
    factors = jnp.concatenate([f1.T, f2.T], axis=0)
    cot = cot[0].reshape(RES * 128, Z)
    row, right, x = call(
        project_kernel,
        [shape((G, 512, S), BF16), shape((256, S), BF16), shape((RES, S, F), BF16)],
        x,
        factors,
        cot,
        scratch=[
            pltpu.VMEM((S * RES, F), BF16),
            pltpu.VMEM((2 * C, F), BF16),
            pltpu.VMEM((RES * 128, Z), F32),
            pltpu.VMEM((2, S * RES, 128), F32),
            pltpu.SemaphoreType.DMA((3,)),
        ],
        flops=33554432,
        hbm=True,
        limit=210,
    )
    row = exchange(row, ROW)
    col, grads, weight = call(
        right_kernel,
        [shape((G, 512, S), BF16), shape((1024, 1024), BF16), shape((128, 1024), BF16)],
        row,
        right,
        w,
        scratch=[pltpu.VMEM((1024, 128), F32)],
        flops=2 * 2 * 1024 * 1024 * 128,
    )
    col = exchange(col, COL)
    back, gout = call(
        left_kernel,
        [shape((G, 512, 128), BF16), shape((1024, 128), BF16)],
        row,
        col,
        grads,
        weight,
        scratch=[pltpu.VMEM((1024, 1024), BF16)],
        flops=4 * 2 * 1024 * 1024 * 128,
    )
    back = exchange(back, ROW)
    right, gr = call(
        right_factor_kernel, [shape((256, S), BF16), shape((C, F), F32)], col, x, flops=33554432
    )
    left, tail = call(
        left_factor_kernel,
        [shape((256, S), BF16), shape((32, 40, 128), BF16)],
        back,
        gr,
        x,
        gout,
        flops=16777216,
    )
    (update,) = call(update_kernel, [shape((RES * 128, Z), F32)], back)
    (msa,) = call(msa_kernel, [shape((RES, S, F), BF16)], left, right, factors, flops=33554432)
    tail = exchange(tail, NEAR)
    (tail,) = call(sum_kernel, [shape((16, 40, 128), BF16)], tail)
    tail = exchange(tail, FAR)
    (tail,) = call(sum_kernel, [shape((32, 40, 128), BF16)], tail)
    tail = exchange(tail, NEAR)
    gl, gr, gout = call(
        final_kernel,
        [shape((C, F), F32), shape((C, F), F32), shape((1024, 128), F32)],
        tail,
        scratch=[pltpu.VMEM((1024, 128), F32)],
    )
    return update.reshape(1, RES, 128, Z), msa.transpose(1, 0, 2)[None], gl.T, gr.T, gout


def solution(mesh):
    split = Mesh(mesh.devices.reshape(4, 4, 2, 4, 2, 2), ("yh", "x", "core", "zh", "zl", "yl"))
    in_specs = (P(DP, None, AXIAL, None), P(), P(), P(), P(DP, AXIAL, None, None))
    out_specs = (P(DP, AXIAL, None, None), P(DP, None, AXIAL, None), P(), P(), P())
    return jax.shard_map(per_device, mesh=split, in_specs=in_specs, out_specs=out_specs, check_vma=False)
```

time: 120 us -> 109 us (0.908)
  blocking collectives: 92 us -> 70 us
  waiting for transfers between devices: 4.51 us -> 12 us
  starting transfers between devices: 6.85 us -> 11.8 us
  local copies, waits for them, and re-layouts: 4.64 us -> 1.09 us
    all_to_all x7 -> x4, blocking collectives: 92 us -> 70 us  [exchange(): return lax.all_to_all(x, axes, split_axis=0, concat_axis=0, tiled=True)]
    all_to_all x1 -> x2, waiting for transfers between devices: 4.51 us -> 12 us  [exchange(): return lax.all_to_all(x, axes, split_axis=0, concat_axis=0, tiled=True)]
    all_to_all x1 -> x2, starting transfers between devices: 6.85 us -> 11.8 us  [exchange(): return lax.all_to_all(x, axes, split_axis=0, concat_axis=0, tiled=True)]
    unnamed x12 -> x3, local copies, waits for them, and re-layouts: 4.64 us -> 1.09 us
  transfers between devices with their start and end apart: 1 -> 2, of which waited for: 1 -> 2; matrix products, arithmetic and copies ran while one was open for 1% -> 1% of each run, Pallas kernels for 1% -> 1%
where the time goes in v2:
time: 109 us; the launch traced here: 108 us
  blocking collectives  70 us (64%)
  waiting for transfers between devices  12 us (11%)
  Pallas kernels  11.9 us (11%)
  starting transfers between devices  11.8 us (11%)
  local copies, waits for them, and re-layouts  1.09 us (1%)
    all_to_all x4, blocking collectives, exchange(): return lax.all_to_all(x, axes, split_axis=0, concat_axis=0, tiled=True)  70 us
    all_to_all x2, waiting for transfers between devices, exchange(): return lax.all_to_all(x, axes, split_axis=0, concat_axis=0, tiled=True)  12 us
    pallas_call x10, Pallas kernels, call(): pl.pallas_call(kernel, out_shape=out, in_specs=[pl.BlockSpec(memory_space...  11.9 us
    all_to_all x2, starting transfers between devices, exchange(): return lax.all_to_all(x, axes, split_axis=0, concat_axis=0, tiled=True)  11.8 us
  transfers between devices with their start and end apart: 2, of which 2 were waited for; matrix products, arithmetic and copies ran while one was open for 1% of the time, Pallas kernels for 1%

profile of v2, /device:TPU:1, one launch (start us, length us, event | category | flops | bytes accessed | tf_op | source)
XLA Modules:
  0.0 108.2 jit_solution(17081501332432284725)
XLA Ops:
  0.6 0.0 copy-start
  0.6 0.8 pad_maximum_fusion.f_hbm.f_ref
  1.4 1.7 %shard_map.92 = (bf16[4,512,128]{2,1,0:T(8,128)(2,1)S(1)}, bf16[256,128]{1,0:T(8,128)(2,1)S(1)}, bf16[8,128,256]{2,1,0:T(8,128)(2,1)S(1)}) custom-call(bf16[1024,256]{1,0:T(8,128)(2,1)} %bitcast.11, bf16[64,256]{1,0:T(8,128)(2,1)S(1)} %pad_maximum_fusion.f_hbm.f_ref, f32[1024,128]{1,0:T(8,128)} %bitcast.12), custom_call_target="tpu_custom_call" | custom-call | flops 33554432 | bytes 2195456 | tf_op jit(solution)/shard_map/pallas_call | solution.py:45
  3.2 11.0 %all_to_all.30.row_ref = bf16[4,512,128]{2,1,0:T(8,128)(2,1)S(1)} all-to-all(bf16[4,512,128]{2,1,0:T(8,128)(2,1)S(1)} %get-tuple-element.20), channel_id=1, replica_groups=mesh['yh'=4,'x'=4,'core'=2,'zh'=4,'zl'=2,'yl'=2] {'zl','yl'}, dimensions={0} | all-to-all | bytes 1048576 | tf_op jit(solution)/shard_map/all_to_all | solution.py:61
  14.1 0.0 copy-done
  14.1 2.6 %shard_map.93 = (bf16[4,512,128]{2,1,0:T(8,128)(2,1)S(1)}, bf16[1024,1024]{1,0:T(8,128)(2,1)S(1)}, bf16[128,1024]{1,0:T(8,128)(2,1)S(1)}) custom-call(bf16[4,512,128]{2,1,0:T(8,128)(2,1)S(1)} %all_to_all.30.row_ref, bf16[256,128]{1,0:T(8,128)(2,1)S(1)} %get-tuple-element.21.right_ref, bf16[1024,128]{1,0:T(8,128)(2,1)S(1)} %copy-done), custom_call_target="tpu_custom_call" | custom-call | flops 536870912 | bytes 3735552 | tf_op jit(solution)/shard_map/pallas_call | solution.py:45
  16.7 22.2 %all_to_all.31.col_ref = bf16[4,512,128]{2,1,0:T(8,128)(2,1)S(1)} all-to-all(bf16[4,512,128]{2,1,0:T(8,128)(2,1)S(1)} %get-tuple-element.22), channel_id=1, replica_groups=mesh['yh'=4,'x'=4,'core'=2,'zh'=4,'zl'=2,'yl'=2] {'zh'}, dimensions={0} | all-to-all | bytes 1048576 | tf_op jit(solution)/shard_map/all_to_all | solution.py:61
  38.9 3.8 %shard_map.94 = (bf16[4,512,128]{2,1,0:T(8,128)(2,1)}, bf16[1024,128]{1,0:T(8,128)(2,1)S(1)}) custom-call(bf16[4,512,128]{2,1,0:T(8,128)(2,1)S(1)} %all_to_all.30.row_ref, bf16[4,512,128]{2,1,0:T(8,128)(2,1)S(1)} %all_to_all.31.col_ref, bf16[1024,1024]{1,0:T(8,128)(2,1)S(1)} %get-tuple-element.23.grads_ref, bf16[128,1024]{1,0:T(8,128)(2,1)S(1)} %get-tuple-element.24.weight_ref), custom_call_target="tpu_custom_call" | custom-call | flops 1073741824 | bytes 4194304 | tf_op jit(solution)/shard_map/pallas_call | solution.py:45
  42.8 5.6 %all-to-all-start.2 = ((bf16[4,512,128]{2,1,0:T(8,128)(2,1)}), bf16[4,512,128]{2,1,0:T(8,128)(2,1)S(1)}, u32[]{:S(2)}, u32[]{:S(2)}) async-start(bf16[4,512,128]{2,1,0:T(8,128)(2,1)} %get-tuple-element.25), calls=%async_computation.2 | async-start | bytes 1048576 | tf_op jit(solution)/shard_map/all_to_all | solution.py:61
  48.3 0.4 shard_map.96
  48.7 5.8 %all-to-all-done.2.back_ref = bf16[4,512,128]{2,1,0:T(8,128)(2,1)S(1)} async-done(((bf16[4,512,128]{2,1,0:T(8,128)(2,1)}), bf16[4,512,128]{2,1,0:T(8,128)(2,1)S(1)}, u32[]{:S(2)}, u32[]{:S(2)}) %all-to-all-start.2) | async-done | bytes 524320 | tf_op jit(solution)/shard_map/all_to_all | solution.py:61
  54.5 0.2 shard_map.97
  54.7 17.7 %all_to_all.32.in_ref = bf16[32,40,128]{2,1,0:T(8,128)(2,1)S(1)} all-to-all(bf16[32,40,128]{2,1,0:T(8,128)(2,1)S(1)} %get-tuple-element.31), channel_id=1, replica_groups=mesh['yh'=4,'x'=4,'core'=2,'zh'=4,'zl'=2,'yl'=2] {'x','core','zl','yl'}, dimensions={0} | all-to-all | bytes 655360 | tf_op jit(solution)/shard_map/all_to_all | solution.py:61
  72.4 0.1 shard_map.99
  72.5 19.1 %all_to_all.33.in_ref = bf16[16,40,128]{2,1,0:T(8,128)(2,1)S(1)} all-to-all(bf16[16,40,128]{2,1,0:T(8,128)(2,1)S(1)} %shard_map.99), channel_id=1, replica_groups=mesh['yh'=4,'x'=4,'core'=2,'zh'=4,'zl'=2,'yl'=2] {'yh','zh'}, dimensions={0} | all-to-all | bytes 327680 | tf_op jit(solution)/shard_map/all_to_all | solution.py:61
  91.5 0.8 shard_map.100
  92.3 6.3 %all-to-all-start.5 = ((bf16[32,40,128]{2,1,0:T(8,128)(2,1)}), bf16[32,40,128]{2,1,0:T(8,128)(2,1)S(1)}, u32[]{:S(2)}, u32[]{:S(2)}) async-start(bf16[32,40,128]{2,1,0:T(8,128)(2,1)} %shard_map.100), calls=%async_computation.5 | async-start | bytes 655360 | tf_op jit(solution)/shard_map/all_to_all | solution.py:61
  98.6 0.3 shard_map.98
  98.9 1.1 %copy.10 = bf16[1,128,8,256]{3,2,1,0:T(8,128)(2,1)} copy(bf16[1,128,8,256]{3,1,2,0:T(8,128)(2,1)S(1)} %bitcast.10) | data formatting | bytes 1048576
  100.0 0.9 shard_map.95
  100.9 6.2 %all-to-all-done.5.in_ref = bf16[32,40,128]{2,1,0:T(8,128)(2,1)S(1)} async-done(((bf16[32,40,128]{2,1,0:T(8,128)(2,1)}), bf16[32,40,128]{2,1,0:T(8,128)(2,1)S(1)}, u32[]{:S(2)}, u32[]{:S(2)}) %all-to-all-start.5) | async-done | bytes 327712 | tf_op jit(solution)/shard_map/all_to_all | solution.py:61
  107.0 1.1 %shard_map.101 = (f32[32,256]{1,0:T(8,128)}, f32[32,256]{1,0:T(8,128)}, f32[1024,128]{1,0:T(8,128)}) custom-call(bf16[32,40,128]{2,1,0:T(8,128)(2,1)S(1)} %all-to-all-done.5.in_ref), custom_call_target="tpu_custom_call" | custom-call | bytes 917504 | tf_op jit(solution)/shard_map/pallas_call | solution.py:45
Async XLA Ops:
  0.6 13.5 %copy-start = (bf16[1024,128]{1,0:T(8,128)(2,1)S(1)}, bf16[1024,128]{1,0:T(8,128)(2,1)}, u32[]{:S(2)}) copy-start(bf16[1024,128]{1,0:T(8,128)(2,1)} %w_ref.1) | copy-start | bytes 786436
  42.8 11.7 %all-to-all-start.2 = ((bf16[4,512,128]{2,1,0:T(8,128)(2,1)}), bf16[4,512,128]{2,1,0:T(8,128)(2,1)S(1)}, u32[]{:S(2)}, u32[]{:S(2)}) async-start(bf16[4,512,128]{2,1,0:T(8,128)(2,1)} %get-tuple-element.25), calls=%async_computation.2 | async-start | bytes 1048576 | tf_op jit(solution)/shard_map/all_to_all | solution.py:61
  92.3 14.7 %all-to-all-start.5 = ((bf16[32,40,128]{2,1,0:T(8,128)(2,1)}), bf16[32,40,128]{2,1,0:T(8,128)(2,1)S(1)}, u32[]{:S(2)}, u32[]{:S(2)}) async-start(bf16[32,40,128]{2,1,0:T(8,128)(2,1)} %shard_map.100), calls=%async_computation.5 | async-start | bytes 655360 | tf_op jit(solution)/shard_map/all_to_all | solution.py:61

commit v3 on v2

--- a/solution.py
+++ b/solution.py
@@ -10,7 +10,7 @@
 ROW = ("zl", "yl")
 COL = "zh"
 NEAR = ("x", "core", "zl", "yl")
-FAR = ("yh", "zh")
+FAR = ("zh", "yh")
 AXIAL = ("zh", "zl", "yl")
 DP = ("yh", "x", "core")
 
@@ -102,27 +102,15 @@
                 row_ref[b, i * 32 + h * 16 : i * 32 + h * 16 + 16, :] = pair.astype(BF16)
 
 
-def swap_to_channels(o):
-    n = o.shape[0] // C
-    blocks = []
-    for e in range(C):
-        at = e * 32
-        blocks.append(
-            jnp.concatenate([o[i * 32 : i * 32 + 32, at : at + 32] for i in range(n)], axis=1)
-        )
-    return jnp.concatenate(blocks, axis=0)
-
-
-def swap_to_residues(g):
-    n = g.shape[1] // 32
-    rows = []
-    for i in range(n):
-        rows.append(
-            jnp.concatenate(
-                [g[e * 32 : e * 32 + 32, i * 32 : i * 32 + 32] for e in range(C)], axis=1
-            )
-        )
-    return jnp.concatenate(rows, axis=0)
+def swap_blocks(blocks):
+    lane = lax.broadcasted_iota(jnp.int32, (32, 128), 1)
+    low, even = (lane & 64) == 0, (lane & 32) == 0
+    a, b, c, d = blocks
+    a, c = jnp.where(low, a, pltpu.roll(c, 64, 1)), jnp.where(low, pltpu.roll(a, 64, 1), c)
+    b, d = jnp.where(low, b, pltpu.roll(d, 64, 1)), jnp.where(low, pltpu.roll(b, 64, 1), d)
+    a, b = jnp.where(even, a, pltpu.roll(b, 32, 1)), jnp.where(even, pltpu.roll(a, 96, 1), b)
+    c, d = jnp.where(even, c, pltpu.roll(d, 32, 1)), jnp.where(even, pltpu.roll(c, 96, 1), d)
+    return a, b, c, d
 
 
 def right_kernel(row_ref, right_ref, w_ref, col_ref, grads_ref, weight_ref, wide):
@@ -131,9 +119,12 @@
     weight_ref[...] = weight.T.astype(BF16)
     weight = weight.astype(BF16)
     for b in range(G):
-        grads_ref[b * 256 : b * 256 + 256, :] = swap_to_residues(
-            nt(weight, row_ref[b, 0:256, :]).astype(BF16)
-        )
+        for at in range(0, 1024, 128):
+            grad = nt(weight[at : at + 128], row_ref[b, 0:256, :]).astype(BF16)
+            for i in range(RES):
+                grads_ref[b * 256 + i * 32 : b * 256 + i * 32 + 32, at : at + 128] = jnp.concatenate(
+                    [grad[e * 32 : e * 32 + 32, i * 32 : i * 32 + 32] for e in range(4)], axis=1
+                )
     lefts = jnp.concatenate([row_ref[b, 256:512, :] for b in range(G)], axis=0)
     rg = (tn(lefts, grads_ref[...]) * (1.0 / S)).T.reshape(C, G, RES, S)
     for a in range(G):
@@ -146,26 +137,31 @@
         [col_ref[a, 256:512, :].astype(F32).reshape(C, RES, S) for a in range(G)], axis=1
     ).reshape(C * G * RES, S).astype(BF16)
     for b in range(G):
-        outer = swap_to_channels((nt(row_ref[b, 256:512, :], right) * (1.0 / S)).astype(BF16))
-        outers[:, b * 256 : b * 256 + 256] = outer
-        out_ref[b, 0:256, :] = nn(weight_ref[...], outer).T.astype(BF16)
+        outer = (nt(row_ref[b, 256:512, :], right) * (1.0 / S)).astype(BF16)
+        for i in range(0, 256, 128):
+            for e in range(0, 1024, 128):
+                blocks = [outer[i + q : i + q + 32, e : e + 128] for q in range(0, 128, 32)]
+                for q, block in enumerate(swap_blocks(blocks)):
+                    outers[e + q * 32 : e + q * 32 + 32, b * 256 + i : b * 256 + i + 128] = block
+    for b in range(G):
         out_ref[b, 256:512, :] = (nn(grads_ref[b * 256 : b * 256 + 256, :], right) * (1.0 / S)).astype(BF16)
+    update = nn(weight_ref[...], outers[...])
+    for b in range(G):
+        out_ref[b, 0:256, :] = update[:, b * 256 : b * 256 + 256].T.astype(BF16)
     cot = jnp.concatenate([row_ref[b, 0:256, :] for b in range(G)], axis=0)
     gout_ref[...] = nn(outers[...], cot).astype(BF16)
 
 
-def right_factor_kernel(col_ref, x_ref, right_ref, gr_ref):
+def factor_kernel(back_ref, col_ref, x_ref, gout_ref, left_ref, right_ref, tail_ref):
+    left = sum(back_ref[b, 256:512, :].astype(F32) for b in range(G)).astype(BF16)
+    left_ref[...] = left
     right = sum(col_ref[a, 0:256, :].astype(F32) for a in range(G)).astype(BF16)
     right = tn(channel_major(), right).astype(BF16)
     right_ref[...] = right
-    gr_ref[...] = sum(nn(right[i * C : i * C + C], x_ref[i]) for i in range(RES))
-
-
-def left_factor_kernel(back_ref, gr_ref, x_ref, gout_ref, left_ref, tail_ref):
-    left = sum(back_ref[b, 256:512, :].astype(F32) for b in range(G)).astype(BF16)
-    left_ref[...] = left
-    gl = sum(nn(left[i * C : i * C + C], x_ref[i]) for i in range(RES))
-    total = jnp.concatenate([gl, gr_ref[...]], axis=0)
+    total = jnp.zeros((2 * C, F), F32)
+    for i in range(RES):
+        both = jnp.concatenate([left[i * C : i * C + C], right[i * C : i * C + C]], axis=0)
+        total = total + nn(both, x_ref[i])
     rows = jnp.concatenate([total[:, 0:128], total[:, 128:256]], axis=0)
     pad = jnp.zeros((4, 128), F32)
     for k in range(C):
@@ -257,17 +253,14 @@
         flops=4 * 2 * 1024 * 1024 * 128,
     )
     back = exchange(back, ROW)
-    right, gr = call(
-        right_factor_kernel, [shape((256, S), BF16), shape((C, F), F32)], col, x, flops=33554432
-    )
-    left, tail = call(
-        left_factor_kernel,
-        [shape((256, S), BF16), shape((32, 40, 128), BF16)],
+    left, right, tail = call(
+        factor_kernel,
+        [shape((256, S), BF16), shape((256, S), BF16), shape((32, 40, 128), BF16)],
         back,
-        gr,
+        col,
         x,
         gout,
-        flops=16777216,
+        flops=33554432,
     )
     (update,) = call(update_kernel, [shape((RES * 128, Z), F32)], back)
     (msa,) = call(msa_kernel, [shape((RES, S, F), BF16)], left, right, factors, flops=33554432)

time: 109 us -> 106 us (0.972)
  blocking collectives: 70 us -> 80.6 us
  waiting for transfers between devices: 12 us -> 6.17 us
  starting transfers between devices: 11.8 us -> 6.33 us
  Pallas kernels: 11.9 us -> 10 us
    all_to_all x4 -> x5, blocking collectives: 70 us -> 80.6 us  [exchange(): return lax.all_to_all(x, axes, split_axis=0, concat_axis=0, tiled=True)]
    all_to_all x2 -> x1, waiting for transfers between devices: 12 us -> 6.17 us  [exchange(): return lax.all_to_all(x, axes, split_axis=0, concat_axis=0, tiled=True)]
    all_to_all x2 -> x1, starting transfers between devices: 11.8 us -> 6.33 us  [exchange(): return lax.all_to_all(x, axes, split_axis=0, concat_axis=0, tiled=True)]
    pallas_call x10 -> x9, Pallas kernels: 11.9 us -> 10 us  [call(): pl.pallas_call(kernel, out_shape=out, in_specs=[pl.BlockSpec(memory_space...]
  transfers between devices with their start and end apart: 2 -> 1, of which waited for: 2 -> 1; matrix products, arithmetic and copies ran while one was open for 1% -> 1% of each run, Pallas kernels for 1% -> 1%
where the time goes in v3:
time: 106 us
  blocking collectives  80.6 us (76%)
  Pallas kernels  10 us (9%)
  starting transfers between devices  6.33 us (6%)
  waiting for transfers between devices  6.17 us (6%)
  local copies, waits for them, and re-layouts  1.09 us (1%)
    all_to_all x5, blocking collectives, exchange(): return lax.all_to_all(x, axes, split_axis=0, concat_axis=0, tiled=True)  80.6 us
    pallas_call x9, Pallas kernels, call(): pl.pallas_call(kernel, out_shape=out, in_specs=[pl.BlockSpec(memory_space...  10 us
    all_to_all x1, starting transfers between devices, exchange(): return lax.all_to_all(x, axes, split_axis=0, concat_axis=0, tiled=True)  6.33 us
    all_to_all x1, waiting for transfers between devices, exchange(): return lax.all_to_all(x, axes, split_axis=0, concat_axis=0, tiled=True)  6.17 us
  transfers between devices with their start and end apart: 1, of which 1 were waited for; matrix products, arithmetic and copies ran while one was open for 1% of the time, Pallas kernels for 1%

profile of v3, /device:TPU:1, one launch (start us, length us, event | category | flops | bytes accessed | tf_op | source)
XLA Modules:
  0.0 105.7 jit_solution(13579424803131426021)
XLA Ops:
  0.6 0.0 copy-start
  0.6 0.8 pad_maximum_fusion.f_hbm.f_ref
  1.4 1.7 %shard_map.92 = (bf16[4,512,128]{2,1,0:T(8,128)(2,1)S(1)}, bf16[256,128]{1,0:T(8,128)(2,1)S(1)}, bf16[8,128,256]{2,1,0:T(8,128)(2,1)S(1)}) custom-call(bf16[1024,256]{1,0:T(8,128)(2,1)} %bitcast.11, bf16[64,256]{1,0:T(8,128)(2,1)S(1)} %pad_maximum_fusion.f_hbm.f_ref, f32[1024,128]{1,0:T(8,128)} %bitcast.12), custom_call_target="tpu_custom_call" | custom-call | flops 33554432 | bytes 2195456 | tf_op jit(solution)/shard_map/pallas_call | solution.py:45
  3.2 11.0 %all_to_all.30.row_ref = bf16[4,512,128]{2,1,0:T(8,128)(2,1)S(1)} all-to-all(bf16[4,512,128]{2,1,0:T(8,128)(2,1)S(1)} %get-tuple-element.19), channel_id=1, replica_groups=mesh['yh'=4,'x'=4,'core'=2,'zh'=4,'zl'=2,'yl'=2] {'zl','yl'}, dimensions={0} | all-to-all | bytes 1048576 | tf_op jit(solution)/shard_map/all_to_all | solution.py:61
  14.1 0.0 copy-done
  14.1 2.6 %shard_map.93 = (bf16[4,512,128]{2,1,0:T(8,128)(2,1)S(1)}, bf16[1024,1024]{1,0:T(8,128)(2,1)S(1)}, bf16[128,1024]{1,0:T(8,128)(2,1)S(1)}) custom-call(bf16[4,512,128]{2,1,0:T(8,128)(2,1)S(1)} %all_to_all.30.row_ref, bf16[256,128]{1,0:T(8,128)(2,1)S(1)} %get-tuple-element.20.right_ref, bf16[1024,128]{1,0:T(8,128)(2,1)S(1)} %copy-done), custom_call_target="tpu_custom_call" | custom-call | flops 536870912 | bytes 3735552 | tf_op jit(solution)/shard_map/pallas_call | solution.py:45
  16.7 22.2 %all_to_all.31.col_ref = bf16[4,512,128]{2,1,0:T(8,128)(2,1)S(1)} all-to-all(bf16[4,512,128]{2,1,0:T(8,128)(2,1)S(1)} %get-tuple-element.21), channel_id=1, replica_groups=mesh['yh'=4,'x'=4,'core'=2,'zh'=4,'zl'=2,'yl'=2] {'zh'}, dimensions={0} | all-to-all | bytes 1048576 | tf_op jit(solution)/shard_map/all_to_all | solution.py:61
  38.9 2.2 %shard_map.94 = (bf16[4,512,128]{2,1,0:T(8,128)(2,1)S(1)}, bf16[1024,128]{1,0:T(8,128)(2,1)S(1)}) custom-call(bf16[4,512,128]{2,1,0:T(8,128)(2,1)S(1)} %all_to_all.30.row_ref, bf16[4,512,128]{2,1,0:T(8,128)(2,1)S(1)} %all_to_all.31.col_ref, bf16[1024,1024]{1,0:T(8,128)(2,1)S(1)} %get-tuple-element.22.grads_ref, ...), custom_call_target="tpu_custom_call" | custom-call | flops 1073741824 | bytes 4194304 | tf_op jit(solution)/shard_map/pallas_call | solution.py:45
  41.1 11.3 %all_to_all.32.back_ref = bf16[4,512,128]{2,1,0:T(8,128)(2,1)S(1)} all-to-all(bf16[4,512,128]{2,1,0:T(8,128)(2,1)S(1)} %get-tuple-element.24), channel_id=1, replica_groups=mesh['yh'=4,'x'=4,'core'=2,'zh'=4,'zl'=2,'yl'=2] {'zl','yl'}, dimensions={0} | all-to-all | bytes 1048576 | tf_op jit(solution)/shard_map/all_to_all | solution.py:61
  52.4 0.4 shard_map.96
  52.8 17.0 %all_to_all.33.in_ref = bf16[32,40,128]{2,1,0:T(8,128)(2,1)S(1)} all-to-all(bf16[32,40,128]{2,1,0:T(8,128)(2,1)S(1)} %get-tuple-element.29), channel_id=1, replica_groups=mesh['yh'=4,'x'=4,'core'=2,'zh'=4,'zl'=2,'yl'=2] {'x','core','zl','yl'}, dimensions={0} | all-to-all | bytes 655360 | tf_op jit(solution)/shard_map/all_to_all | solution.py:61
  69.9 0.1 shard_map.98
  69.9 19.1 %all_to_all.34.in_ref = bf16[16,40,128]{2,1,0:T(8,128)(2,1)S(1)} all-to-all(bf16[16,40,128]{2,1,0:T(8,128)(2,1)S(1)} %shard_map.98), channel_id=1, replica_groups=mesh['yh'=4,'x'=4,'core'=2,'zh'=4,'zl'=2,'yl'=2] {'zh','yh'}, dimensions={0} | all-to-all | bytes 327680 | tf_op jit(solution)/shard_map/all_to_all | solution.py:61
  89.0 0.8 shard_map.99
  89.8 6.3 %all-to-all-start.5 = ((bf16[32,40,128]{2,1,0:T(8,128)(2,1)}), bf16[32,40,128]{2,1,0:T(8,128)(2,1)S(1)}, u32[]{:S(2)}, u32[]{:S(2)}) async-start(bf16[32,40,128]{2,1,0:T(8,128)(2,1)} %shard_map.99), calls=%async_computation.5 | async-start | bytes 655360 | tf_op jit(solution)/shard_map/all_to_all | solution.py:61
  96.1 0.3 shard_map.97
  96.5 1.1 %copy.10 = bf16[1,128,8,256]{3,2,1,0:T(8,128)(2,1)} copy(bf16[1,128,8,256]{3,1,2,0:T(8,128)(2,1)S(1)} %bitcast.10) | data formatting | bytes 1048576
  97.5 0.9 shard_map.95
  98.4 6.2 %all-to-all-done.5.in_ref = bf16[32,40,128]{2,1,0:T(8,128)(2,1)S(1)} async-done(((bf16[32,40,128]{2,1,0:T(8,128)(2,1)}), bf16[32,40,128]{2,1,0:T(8,128)(2,1)S(1)}, u32[]{:S(2)}, u32[]{:S(2)}) %all-to-all-start.5) | async-done | bytes 327712 | tf_op jit(solution)/shard_map/all_to_all | solution.py:61
  104.6 1.1 %shard_map.100 = (f32[32,256]{1,0:T(8,128)}, f32[32,256]{1,0:T(8,128)}, f32[1024,128]{1,0:T(8,128)}) custom-call(bf16[32,40,128]{2,1,0:T(8,128)(2,1)S(1)} %all-to-all-done.5.in_ref), custom_call_target="tpu_custom_call" | custom-call | bytes 917504 | tf_op jit(solution)/shard_map/pallas_call | solution.py:45
Async XLA Ops:
  0.6 13.5 %copy-start = (bf16[1024,128]{1,0:T(8,128)(2,1)S(1)}, bf16[1024,128]{1,0:T(8,128)(2,1)}, u32[]{:S(2)}) copy-start(bf16[1024,128]{1,0:T(8,128)(2,1)} %w_ref.1) | copy-start | bytes 786436
  89.8 14.8 %all-to-all-start.5 = ((bf16[32,40,128]{2,1,0:T(8,128)(2,1)}), bf16[32,40,128]{2,1,0:T(8,128)(2,1)S(1)}, u32[]{:S(2)}, u32[]{:S(2)}) async-start(bf16[32,40,128]{2,1,0:T(8,128)(2,1)} %shard_map.99), calls=%async_computation.5 | async-start | bytes 655360 | tf_op jit(solution)/shard_map/all_to_all | solution.py:61

commit v4 on v3

--- a/solution.py
+++ b/solution.py
@@ -10,6 +10,7 @@
 ROW = ("zl", "yl")
 COL = "zh"
 NEAR = ("x", "core", "zl", "yl")
+NEAREST = ("x", "zl", "yl")
 FAR = ("zh", "yh")
 AXIAL = ("zh", "zl", "yl")
 DP = ("yh", "x", "core")
@@ -38,7 +39,7 @@
     return dot(a, b, ((0,), (0,)))
 
 
-def call(kernel, out, *args, scratch=(), flops=0, hbm=False, limit=96):
+def call(kernel, out, *args, scratch=(), flops=0, hbm=False, limit=96, aliases=None):
     size = sum(a.size * a.dtype.itemsize for a in args) + sum(
         o.size * o.dtype.itemsize for o in out
     )
@@ -48,6 +49,7 @@
         in_specs=[pl.BlockSpec(memory_space=pltpu.HBM if hbm else pltpu.VMEM)] * len(args),
         out_specs=[pl.BlockSpec(memory_space=pltpu.VMEM)] * len(out),
         scratch_shapes=list(scratch),
+        input_output_aliases=aliases or {},
         compiler_params=pltpu.CompilerParams(vmem_limit_bytes=limit * 1024 * 256),
         cost_estimate=pl.CostEstimate(flops=flops, bytes_accessed=size, transcendentals=0),
     )(*args)
@@ -69,37 +71,40 @@
     return jnp.where(same, 1.0, 0.0).astype(BF16)
 
 
-def project_kernel(x_hbm, f_hbm, cot_hbm, row_ref, right_ref, xt_ref, x_ref, f_ref, cot_ref, wide, sems):
+def pack_kernel(x_hbm, cot_hbm, row_ref, xt_ref, x_ref, cot_ref, wide, sems):
     copies = [
-        pltpu.make_async_copy(f_hbm, f_ref, sems.at[0]),
-        pltpu.make_async_copy(x_hbm, x_ref, sems.at[1]),
-        pltpu.make_async_copy(cot_hbm, cot_ref, sems.at[2]),
+        pltpu.make_async_copy(x_hbm, x_ref, sems.at[0]),
+        pltpu.make_async_copy(cot_hbm, cot_ref, sems.at[1]),
     ]
     for copy in copies:
         copy.start()
-    for copy in copies[:2]:
-        copy.wait()
-    factors = f_ref[...]
+    copies[0].wait()
     for h in range(2):
         wide[h] = x_ref[:, h * 128 : h * 128 + 128].astype(F32)
-    left, right = [], []
     for i in range(RES):
-        x = jnp.concatenate([wide[h, pl.ds(i, S, stride=RES), :] for h in range(2)], axis=1).astype(BF16)
-        xt_ref[i] = x
-        both = nt(factors, x).astype(BF16)
-        left.append(both[:C])
-        right.append(both[C:])
-    left = jnp.concatenate(left, axis=0)
-    for b in range(G):
-        row_ref[b, 256:512, :] = left
-    right_ref[...] = nn(channel_major(), jnp.concatenate(right, axis=0)).astype(BF16)
-    copies[2].wait()
+        for h in range(2):
+            xt_ref[i, :, h * 128 : h * 128 + 128] = wide[h, pl.ds(i, S, stride=RES), :].astype(BF16)
+    copies[1].wait()
     for b in range(G):
         for i in range(RES):
             for h in range(2):
                 at = i * 128 + h * 64 + b * 8
                 pair = jnp.concatenate([cot_ref[at : at + 8, :], cot_ref[at + 32 : at + 40, :]], axis=0)
                 row_ref[b, i * 32 + h * 16 : i * 32 + h * 16 + 16, :] = pair.astype(BF16)
+
+
+def project_kernel(row_in, x_ref, f1_ref, f2_ref, row_ref, right_ref):
+    del row_in
+    factors = jnp.concatenate([f1_ref[...], f2_ref[...]], axis=0)
+    left, right = [], []
+    for i in range(RES):
+        both = nt(factors, x_ref[i]).astype(BF16)
+        left.append(both[:C])
+        right.append(both[C:])
+    left = jnp.concatenate(left, axis=0)
+    for b in range(G):
+        row_ref[b, 256:512, :] = left
+    right_ref[...] = nn(channel_major(), jnp.concatenate(right, axis=0)).astype(BF16)
 
 
 def swap_blocks(blocks):
@@ -152,7 +157,7 @@
     gout_ref[...] = nn(outers[...], cot).astype(BF16)
 
 
-def factor_kernel(back_ref, col_ref, x_ref, gout_ref, left_ref, right_ref, tail_ref):
+def factor_kernel(back_ref, col_ref, x_ref, gout_ref, other_ref, left_ref, right_ref, tail_ref):
     left = sum(back_ref[b, 256:512, :].astype(F32) for b in range(G)).astype(BF16)
     left_ref[...] = left
     right = sum(col_ref[a, 0:256, :].astype(F32) for a in range(G)).astype(BF16)
@@ -163,11 +168,10 @@
         both = jnp.concatenate([left[i * C : i * C + C], right[i * C : i * C + C]], axis=0)
         total = total + nn(both, x_ref[i])
     rows = jnp.concatenate([total[:, 0:128], total[:, 128:256]], axis=0)
-    pad = jnp.zeros((4, 128), F32)
-    for k in range(C):
-        tail_ref[k] = jnp.concatenate(
-            [gout_ref[k * 32 : k * 32 + 32, :].astype(F32), rows[k * 4 : k * 4 + 4], pad], axis=0
-        ).astype(BF16)
+    half = pl.ds(pl.multiple_of(lax.axis_index("core") * 512, 512), 512)
+    gout = gout_ref[half, :].astype(F32) + other_ref[half, :].astype(F32)
+    for k in range(16):
+        tail_ref[k] = jnp.concatenate([gout[k * 32 : k * 32 + 32], rows[k * 8 : k * 8 + 8]], axis=0).astype(BF16)
 
 
 def update_kernel(back_ref, out_ref):
@@ -179,8 +183,8 @@
                 out_ref[at : at + 8, :] = part[i * 32 + a * 8 : i * 32 + a * 8 + 8, :]
 
 
-def msa_kernel(left_ref, right_ref, f_ref, out_ref):
-    factors = f_ref[...]
+def msa_kernel(left_ref, right_ref, f1_ref, f2_ref, out_ref):
+    factors = jnp.concatenate([f1_ref[...], f2_ref[...]], axis=0)
     for i in range(RES):
         both = jnp.concatenate([left_ref[i * C : i * C + C, :], right_ref[i * C : i * C + C, :]], axis=0)
         out_ref[i] = tn(both, factors).astype(BF16)
@@ -198,38 +202,48 @@
 def final_kernel(in_ref, gl_ref, gr_ref, gout_ref, wide):
     scale = 1.0 / 32
     rows = []
-    for e in range(C):
-        part = in_ref[e].astype(F32) * scale
-        wide[e * 32 : e * 32 + 32, :] = part[0:32]
-        rows.append(part[32:36])
+    for k in range(16):
+        at = k // 4 * 8 + k % 4
+        parts = [in_ref[at + core * 4].astype(F32) * scale for core in range(2)]
+        for core in range(2):
+            wide[(core * 16 + k) * 32 : (core * 16 + k) * 32 + 32, :] = parts[core][0:32]
+        rows.append(parts[0][32:40] + parts[1][32:40])
     for h in range(2):
         for q, out in enumerate((gl_ref, gr_ref)):
-            at = h * 16 + q * 8
-            out[:, h * 128 : h * 128 + 128] = jnp.concatenate(rows[at : at + 8], axis=0)
+            at = h * 8 + q * 4
+            out[:, h * 128 : h * 128 + 128] = jnp.concatenate(rows[at : at + 4], axis=0)
     for c in range(C):
         gout_ref[c * 32 : c * 32 + 32, :] = wide[pl.ds(c, 32, stride=32), :]
 
 
 def per_device(x, f1, f2, w, cot):
     x = x[0].reshape(S * RES, F)
-    factors = jnp.concatenate([f1.T, f2.T], axis=0)
+    f1, f2 = f1.T, f2.T
     cot = cot[0].reshape(RES * 128, Z)
-    row, right, x = call(
-        project_kernel,
-        [shape((G, 512, S), BF16), shape((256, S), BF16), shape((RES, S, F), BF16)],
+    row, x = call(
+        pack_kernel,
+        [shape((G, 512, S), BF16), shape((RES, S, F), BF16)],
         x,
-        factors,
         cot,
         scratch=[
             pltpu.VMEM((S * RES, F), BF16),
-            pltpu.VMEM((2 * C, F), BF16),
             pltpu.VMEM((RES * 128, Z), F32),
             pltpu.VMEM((2, S * RES, 128), F32),
-            pltpu.SemaphoreType.DMA((3,)),
+            pltpu.SemaphoreType.DMA((2,)),
         ],
-        flops=33554432,
         hbm=True,
         limit=210,
+        flops=2 * 10**9,
+    )
+    row, right = call(
+        project_kernel,
+        [shape((G, 512, S), BF16), shape((256, S), BF16)],
+        row,
+        x,
+        f1,
+        f2,
+        flops=33554432,
+        aliases={0: 0},
     )
     row = exchange(row, ROW)
     col, grads, weight = call(
@@ -252,19 +266,21 @@
         scratch=[pltpu.VMEM((1024, 1024), BF16)],
         flops=4 * 2 * 1024 * 1024 * 128,
     )
+    other = lax.ppermute(gout, "core", [(0, 1), (1, 0)])
     back = exchange(back, ROW)
     left, right, tail = call(
         factor_kernel,
-        [shape((256, S), BF16), shape((256, S), BF16), shape((32, 40, 128), BF16)],
+        [shape((256, S), BF16), shape((256, S), BF16), shape((16, 40, 128), BF16)],
         back,
         col,
         x,
         gout,
+        other,
         flops=33554432,
     )
     (update,) = call(update_kernel, [shape((RES * 128, Z), F32)], back)
-    (msa,) = call(msa_kernel, [shape((RES, S, F), BF16)], left, right, factors, flops=33554432)
-    tail = exchange(tail, NEAR)
+    (msa,) = call(msa_kernel, [shape((RES, S, F), BF16)], left, right, f1, f2, flops=33554432)
+    tail = exchange(tail, NEAREST)
     (tail,) = call(sum_kernel, [shape((16, 40, 128), BF16)], tail)
     tail = exchange(tail, FAR)
     (tail,) = call(sum_kernel, [shape((32, 40, 128), BF16)], tail)

time: 106 us -> 105 us (level)
  blocking collectives: 80.6 us -> 65.5 us
  starting transfers between devices: 6.33 us -> 18.9 us
  waiting for transfers between devices: 6.17 us -> 7.31 us
    all_to_all x5 -> x4, blocking collectives: 80.6 us -> 65.5 us  [exchange(): return lax.all_to_all(x, axes, split_axis=0, concat_axis=0, tiled=True)]
    all_to_all x1 -> x2, starting transfers between devices: 6.33 us -> 13.2 us  [exchange(): return lax.all_to_all(x, axes, split_axis=0, concat_axis=0, tiled=True)]
    ppermute x0 -> x1, starting transfers between devices: none -> 5.68 us  [per_device(): other = lax.ppermute(gout, 'core', [(0, 1), (1, 0)])]
    ppermute x0 -> x1, waiting for transfers between devices: none -> 1.14 us  [per_device(): other = lax.ppermute(gout, 'core', [(0, 1), (1, 0)])]
    pallas_call x9 -> x10, Pallas kernels: 10 us -> 10.9 us  [call(): pl.pallas_call(kernel, out_shape=out, in_specs=[pl.BlockSpec(memory_space...]
    all_to_all x1 -> x2, waiting for transfers between devices: 6.17 us -> 6.17 us  [exchange(): return lax.all_to_all(x, axes, split_axis=0, concat_axis=0, tiled=True)]
  transfers between devices with their start and end apart: 1 -> 3, of which waited for: 1 -> 2; matrix products, arithmetic and copies ran while one was open for 1% -> 1% of each run, Pallas kernels for 1% -> 1%
where the time goes in v4:
time: 105 us; the launch traced here: 104 us
  blocking collectives  65.5 us (62%)
  starting transfers between devices  18.9 us (18%)
  Pallas kernels  10.9 us (10%)
  waiting for transfers between devices  7.31 us (7%)
  local copies, waits for them, and re-layouts  1.1 us (1%)
    all_to_all x4, blocking collectives, exchange(): return lax.all_to_all(x, axes, split_axis=0, concat_axis=0, tiled=True)  65.5 us
    all_to_all x2, starting transfers between devices, exchange(): return lax.all_to_all(x, axes, split_axis=0, concat_axis=0, tiled=True)  13.2 us
    pallas_call x10, Pallas kernels, call(): pl.pallas_call(kernel, out_shape=out, in_specs=[pl.BlockSpec(memory_space...  10.9 us
    all_to_all x2, waiting for transfers between devices, exchange(): return lax.all_to_all(x, axes, split_axis=0, concat_axis=0, tiled=True)  6.17 us
    ppermute x1, starting transfers between devices, per_device(): other = lax.ppermute(gout, 'core', [(0, 1), (1, 0)])  5.68 us
  transfers between devices with their start and end apart: 3, of which 2 were waited for; matrix products, arithmetic and copies ran while one was open for 1% of the time, Pallas kernels for 1%

profile of v4, /device:TPU:1, one launch (start us, length us, event | category | flops | bytes accessed | tf_op | source)
XLA Modules:
  0.0 104.4 jit_solution(6076914441551922056)
XLA Ops:
  0.6 0.0 copy-start
  0.6 0.0 copy-start.1
  0.7 1.4 %shard_map.92 = (bf16[4,512,128]{2,1,0:T(8,128)(2,1)S(1)}, bf16[8,128,256]{2,1,0:T(8,128)(2,1)S(1)}) custom-call(bf16[1024,256]{1,0:T(8,128)(2,1)} %bitcast.16, f32[1024,128]{1,0:T(8,128)} %bitcast.17), custom_call_target="tpu_custom_call" | custom-call | flops 2000000000 | bytes 2097152 | tf_op jit(solution)/shard_map/pallas_call | solution.py:46
  2.0 0.0 copy-start.2
  2.1 0.0 copy-done
  2.1 0.5 shard_map.93
  2.6 11.0 %all_to_all.30.row_ref = bf16[4,512,128]{2,1,0:T(8,128)(2,1)S(1)} all-to-all(bf16[4,512,128]{2,1,0:T(8,128)(2,1)S(1)} %get-tuple-element.22), channel_id=1, replica_groups=mesh['yh'=4,'x'=4,'core'=2,'zh'=4,'zl'=2,'yl'=2] {'zl','yl'}, dimensions={0} | all-to-all | bytes 1048576 | tf_op jit(solution)/shard_map/all_to_all | solution.py:63
  13.6 2.6 %shard_map.94 = (bf16[4,512,128]{2,1,0:T(8,128)(2,1)S(1)}, bf16[1024,1024]{1,0:T(8,128)(2,1)S(1)}, bf16[128,1024]{1,0:T(8,128)(2,1)S(1)}) custom-call(bf16[4,512,128]{2,1,0:T(8,128)(2,1)S(1)} %all_to_all.30.row_ref, bf16[256,128]{1,0:T(8,128)(2,1)S(1)} %get-tuple-element.23.right_ref, bf16[1024,128]{1,0:T(8,128)(2,1)S(1)} %copy-done.2), custom_call_target="tpu_custom_call" | custom-call | flops 536870912 | bytes 3735552 | tf_op jit(solution)/shard_map/pallas_call | solution.py:46
  16.2 22.2 %all_to_all.31.col_ref = bf16[4,512,128]{2,1,0:T(8,128)(2,1)S(1)} all-to-all(bf16[4,512,128]{2,1,0:T(8,128)(2,1)S(1)} %get-tuple-element.24), channel_id=1, replica_groups=mesh['yh'=4,'x'=4,'core'=2,'zh'=4,'zl'=2,'yl'=2] {'zh'}, dimensions={0} | all-to-all | bytes 1048576 | tf_op jit(solution)/shard_map/all_to_all | solution.py:63
  38.3 2.9 %shard_map.95 = (bf16[4,512,128]{2,1,0:T(8,128)(2,1)}, bf16[1024,128]{1,0:T(8,128)(2,1)S(1)}) custom-call(bf16[4,512,128]{2,1,0:T(8,128)(2,1)S(1)} %all_to_all.30.row_ref, bf16[4,512,128]{2,1,0:T(8,128)(2,1)S(1)} %all_to_all.31.col_ref, bf16[1024,1024]{1,0:T(8,128)(2,1)S(1)} %get-tuple-element.25.grads_ref, bf16[128,1024]{1,0:T(8,128)(2,1)S(1)} %get-tuple-element.26.weight_ref), custom_call_target="tpu_custom_call" | custom-call | flops 1073741824 | bytes 4194304 | tf_op jit(solution)/shard_map/pallas_call | solution.py:46
  41.2 5.6 %all-to-all-start.2 = ((bf16[4,512,128]{2,1,0:T(8,128)(2,1)}), bf16[4,512,128]{2,1,0:T(8,128)(2,1)S(1)}, u32[]{:S(2)}, u32[]{:S(2)}) async-start(bf16[4,512,128]{2,1,0:T(8,128)(2,1)} %get-tuple-element.27), calls=%async_computation.2 | async-start | bytes 1048576 | tf_op jit(solution)/shard_map/all_to_all | solution.py:63
  46.8 5.7 %collective-permute-start = (bf16[1024,128]{1,0:T(8,128)(2,1)S(1)}, bf16[1024,128]{1,0:T(8,128)(2,1)S(1)}, u32[]{:S(2)}, u32[]{:S(2)}) collective-permute-start(bf16[1024,128]{1,0:T(8,128)(2,1)S(1)} %get-tuple-element.28.gout_ref), channel_id=1, source_target_pairs={{0,16},{16,0},{1,17},{17,1},{2,18},{18,2},{3,19},{19,3},{4,20},{20... | collective-permute-start | bytes 786440 | tf_op jit(solution)/shard_map/ppermute | solution.py:269
  52.5 1.1 %collective-permute-done.other_ref = bf16[1024,128]{1,0:T(8,128)(2,1)S(1)} collective-permute-done((bf16[1024,128]{1,0:T(8,128)(2,1)S(1)}, bf16[1024,128]{1,0:T(8,128)(2,1)S(1)}, u32[]{:S(2)}, u32[]{:S(2)}) %collective-permute-start) | collective-permute-done | bytes 262176 | tf_op jit(solution)/shard_map/ppermute | solution.py:269
  53.6 0.0 all-to-all-done.2.back_ref
  53.6 0.4 shard_map.97
  54.1 12.4 %all_to_all.32.in_ref = bf16[16,40,128]{2,1,0:T(8,128)(2,1)S(1)} all-to-all(bf16[16,40,128]{2,1,0:T(8,128)(2,1)S(1)} %get-tuple-element.31), channel_id=1, replica_groups=mesh['yh'=4,'x'=4,'core'=2,'zh'=4,'zl'=2,'yl'=2] {'x','zl','yl'}, dimensions={0} | all-to-all | bytes 327680 | tf_op jit(solution)/shard_map/all_to_all | solution.py:63
  66.5 19.9 %all_to_all.33.in_ref = bf16[16,40,128]{2,1,0:T(8,128)(2,1)S(1)} all-to-all(bf16[16,40,128]{2,1,0:T(8,128)(2,1)S(1)} %shard_map.99), channel_id=1, replica_groups=mesh['yh'=4,'x'=4,'core'=2,'zh'=4,'zl'=2,'yl'=2] {'zh','yh'}, dimensions={0} | all-to-all | bytes 327680 | tf_op jit(solution)/shard_map/all_to_all | solution.py:63
  86.4 0.8 shard_map.100
  87.2 7.6 %all-to-all-start.5 = ((bf16[32,40,128]{2,1,0:T(8,128)(2,1)}), bf16[32,40,128]{2,1,0:T(8,128)(2,1)S(1)}, u32[]{:S(2)}, u32[]{:S(2)}) async-start(bf16[32,40,128]{2,1,0:T(8,128)(2,1)} %shard_map.100), calls=%async_computation.5 | async-start | bytes 655360 | tf_op jit(solution)/shard_map/all_to_all | solution.py:63
  94.8 0.3 shard_map.98
  95.2 1.1 %copy.11 = bf16[1,128,8,256]{3,2,1,0:T(8,128)(2,1)} copy(bf16[1,128,8,256]{3,1,2,0:T(8,128)(2,1)S(1)} %bitcast.10) | data formatting | bytes 1048576
  96.2 0.9 shard_map.96
  97.1 6.2 %all-to-all-done.5.in_ref = bf16[32,40,128]{2,1,0:T(8,128)(2,1)S(1)} async-done(((bf16[32,40,128]{2,1,0:T(8,128)(2,1)}), bf16[32,40,128]{2,1,0:T(8,128)(2,1)S(1)}, u32[]{:S(2)}, u32[]{:S(2)}) %all-to-all-start.5) | async-done | bytes 327712 | tf_op jit(solution)/shard_map/all_to_all | solution.py:63
  103.3 1.1 %shard_map.101 = (f32[32,256]{1,0:T(8,128)}, f32[32,256]{1,0:T(8,128)}, f32[1024,128]{1,0:T(8,128)}) custom-call(bf16[32,40,128]{2,1,0:T(8,128)(2,1)S(1)} %all-to-all-done.5.in_ref), custom_call_target="tpu_custom_call" | custom-call | bytes 917504 | tf_op jit(solution)/shard_map/pallas_call | solution.py:46
  (3 shorter events, 0.0 us)
Async XLA Ops:
  0.6 1.4 %copy-start = (bf16[256,32]{0,1:T(8,128)(2,1)S(1)}, bf16[256,32]{0,1:T(8,128)(2,1)}, u32[]{:S(2)}) copy-start(bf16[256,32]{0,1:T(8,128)(2,1)} %param.6) | copy-start | bytes 49156
  0.6 1.4 %copy-start.1 = (bf16[256,32]{0,1:T(8,128)(2,1)S(1)}, bf16[256,32]{0,1:T(8,128)(2,1)}, u32[]{:S(2)}) copy-start(bf16[256,32]{0,1:T(8,128)(2,1)} %param.7) | copy-start | bytes 49156
  2.0 11.5 %copy-start.2 = (bf16[1024,128]{1,0:T(8,128)(2,1)S(1)}, bf16[1024,128]{1,0:T(8,128)(2,1)}, u32[]{:S(2)}) copy-start(bf16[1024,128]{1,0:T(8,128)(2,1)} %w_ref.1) | copy-start | bytes 786436
  41.2 12.4 %all-to-all-start.2 = ((bf16[4,512,128]{2,1,0:T(8,128)(2,1)}), bf16[4,512,128]{2,1,0:T(8,128)(2,1)S(1)}, u32[]{:S(2)}, u32[]{:S(2)}) async-start(bf16[4,512,128]{2,1,0:T(8,128)(2,1)} %get-tuple-element.27), calls=%async_computation.2 | async-start | bytes 1048576 | tf_op jit(solution)/shard_map/all_to_all | solution.py:63
  46.8 6.8 %collective-permute-start = (bf16[1024,128]{1,0:T(8,128)(2,1)S(1)}, bf16[1024,128]{1,0:T(8,128)(2,1)S(1)}, u32[]{:S(2)}, u32[]{:S(2)}) collective-permute-start(bf16[1024,128]{1,0:T(8,128)(2,1)S(1)} %get-tuple-element.28.gout_ref), channel_id=1, source_target_pairs={{0,16},{16,0},{1,17},{17,1},{2,18},{18,2},{3,19},{19,3},{4,20},{20... | collective-permute-start | bytes 786440 | tf_op jit(solution)/shard_map/ppermute | solution.py:269
  87.2 16.1 %all-to-all-start.5 = ((bf16[32,40,128]{2,1,0:T(8,128)(2,1)}), bf16[32,40,128]{2,1,0:T(8,128)(2,1)S(1)}, u32[]{:S(2)}, u32[]{:S(2)}) async-start(bf16[32,40,128]{2,1,0:T(8,128)(2,1)} %shard_map.100), calls=%async_computation.5 | async-start | bytes 655360 | tf_op jit(solution)/shard_map/all_to_all | solution.py:63

commit v5 on v4

--- a/solution.py
+++ b/solution.py
@@ -72,25 +72,32 @@
 
 
 def pack_kernel(x_hbm, cot_hbm, row_ref, xt_ref, x_ref, cot_ref, wide, sems):
-    copies = [
-        pltpu.make_async_copy(x_hbm, x_ref, sems.at[0]),
-        pltpu.make_async_copy(cot_hbm, cot_ref, sems.at[1]),
-    ]
-    for copy in copies:
-        copy.start()
-    copies[0].wait()
-    for h in range(2):
-        wide[h] = x_ref[:, h * 128 : h * 128 + 128].astype(F32)
-    for i in range(RES):
+    loads = []
+    for k in range(2):
+        part = pl.ds(k * 512, 512)
+        loads.append(pltpu.make_async_copy(x_hbm.at[part], x_ref.at[part], sems.at[k]))
+    for k in range(2):
+        part = pl.ds(k * 512, 512)
+        loads.append(pltpu.make_async_copy(cot_hbm.at[part], cot_ref.at[part], sems.at[2 + k]))
+    for load in loads:
+        load.start()
+    for k in range(2):
+        loads[k].wait()
         for h in range(2):
-            xt_ref[i, :, h * 128 : h * 128 + 128] = wide[h, pl.ds(i, S, stride=RES), :].astype(BF16)
-    copies[1].wait()
-    for b in range(G):
+            wide[h, k * 512 : k * 512 + 512, :] = x_ref[k * 512 : k * 512 + 512, h * 128 : h * 128 + 128].astype(F32)
         for i in range(RES):
             for h in range(2):
-                at = i * 128 + h * 64 + b * 8
-                pair = jnp.concatenate([cot_ref[at : at + 8, :], cot_ref[at + 32 : at + 40, :]], axis=0)
-                row_ref[b, i * 32 + h * 16 : i * 32 + h * 16 + 16, :] = pair.astype(BF16)
+                xt_ref[i, k * 64 : k * 64 + 64, h * 128 : h * 128 + 128] = wide[
+                    h, pl.ds(k * 512 + i, 64, stride=RES), :
+                ].astype(BF16)
+    for k in range(2):
+        loads[2 + k].wait()
+        for b in range(G):
+            for i in range(k * 4, k * 4 + 4):
+                for h in range(2):
+                    at = i * 128 + h * 64 + b * 8
+                    pair = jnp.concatenate([cot_ref[at : at + 8, :], cot_ref[at + 32 : at + 40, :]], axis=0)
+                    row_ref[b, i * 32 + h * 16 : i * 32 + h * 16 + 16, :] = pair.astype(BF16)
 
 
 def project_kernel(row_in, x_ref, f1_ref, f2_ref, row_ref, right_ref):
@@ -137,7 +144,7 @@
         col_ref[a, 256:512, :] = right_ref[...]
 
 
-def left_kernel(row_ref, col_ref, grads_ref, weight_ref, out_ref, gout_ref, outers):
+def left_kernel(row_ref, col_ref, grads_ref, weight_ref, out_ref, update_ref, gout_ref, outers):
     right = jnp.concatenate(
         [col_ref[a, 256:512, :].astype(F32).reshape(C, RES, S) for a in range(G)], axis=1
     ).reshape(C * G * RES, S).astype(BF16)
@@ -149,16 +156,16 @@
                 for q, block in enumerate(swap_blocks(blocks)):
                     outers[e + q * 32 : e + q * 32 + 32, b * 256 + i : b * 256 + i + 128] = block
     for b in range(G):
-        out_ref[b, 256:512, :] = (nn(grads_ref[b * 256 : b * 256 + 256, :], right) * (1.0 / S)).astype(BF16)
+        out_ref[b] = (nn(grads_ref[b * 256 : b * 256 + 256, :], right) * (1.0 / S)).astype(BF16)
     update = nn(weight_ref[...], outers[...])
     for b in range(G):
-        out_ref[b, 0:256, :] = update[:, b * 256 : b * 256 + 256].T.astype(BF16)
+        update_ref[b] = update[:, b * 256 : b * 256 + 256].T.astype(BF16)
     cot = jnp.concatenate([row_ref[b, 0:256, :] for b in range(G)], axis=0)
     gout_ref[...] = nn(outers[...], cot).astype(BF16)
 
 
 def factor_kernel(back_ref, col_ref, x_ref, gout_ref, other_ref, left_ref, right_ref, tail_ref):
-    left = sum(back_ref[b, 256:512, :].astype(F32) for b in range(G)).astype(BF16)
+    left = sum(back_ref[b].astype(F32) for b in range(G)).astype(BF16)
     left_ref[...] = left
     right = sum(col_ref[a, 0:256, :].astype(F32) for a in range(G)).astype(BF16)
     right = tn(channel_major(), right).astype(BF16)
@@ -174,9 +181,27 @@
         tail_ref[k] = jnp.concatenate([gout[k * 32 : k * 32 + 32], rows[k * 8 : k * 8 + 8]], axis=0).astype(BF16)
 
 
-def update_kernel(back_ref, out_ref):
-    for b in range(G):
-        part = back_ref[b, 0:256, :].astype(F32)
+def place():
+    return lax.axis_index("zl") * 2 + lax.axis_index("yl")
+
+
+def split_kernel(in_ref, update_ref, out_ref, *part_refs):
+    sum_kernel(in_ref, out_ref)
+    me = place()
+    for k, ref in enumerate(part_refs):
+        ref[...] = update_ref[lax.bitwise_xor(me, k)]
+
+
+def join_kernel(in_ref, *refs):
+    sum_kernel(in_ref, refs[G])
+    me = place()
+    for k in range(G):
+        refs[G + 1][lax.bitwise_xor(me, k)] = refs[k][...]
+
+
+def update_kernel(update_ref, out_ref):
+    for b in range(G):
+        part = update_ref[b].astype(F32)
         for i in range(RES):
             for a in range(G):
                 at = i * 128 + a * 32 + b * 8
@@ -229,7 +254,7 @@
             pltpu.VMEM((S * RES, F), BF16),
             pltpu.VMEM((RES * 128, Z), F32),
             pltpu.VMEM((2, S * RES, 128), F32),
-            pltpu.SemaphoreType.DMA((2,)),
+            pltpu.SemaphoreType.DMA((4,)),
         ],
         hbm=True,
         limit=210,
@@ -256,9 +281,9 @@
         flops=2 * 2 * 1024 * 1024 * 128,
     )
     col = exchange(col, COL)
-    back, gout = call(
+    back, update, gout = call(
         left_kernel,
-        [shape((G, 512, 128), BF16), shape((1024, 128), BF16)],
+        [shape((G, 256, 128), BF16), shape((G, 256, 128), BF16), shape((1024, 128), BF16)],
         row,
         col,
         grads,
@@ -278,12 +303,17 @@
         other,
         flops=33554432,
     )
-    (update,) = call(update_kernel, [shape((RES * 128, Z), F32)], back)
     (msa,) = call(msa_kernel, [shape((RES, S, F), BF16)], left, right, f1, f2, flops=33554432)
     tail = exchange(tail, NEAREST)
-    (tail,) = call(sum_kernel, [shape((16, 40, 128), BF16)], tail)
+    tail, *updates = call(
+        split_kernel, [shape((16, 40, 128), BF16)] + [shape((256, 128), BF16)] * G, tail, update
+    )
     tail = exchange(tail, FAR)
-    (tail,) = call(sum_kernel, [shape((32, 40, 128), BF16)], tail)
+    updates = [lax.ppermute(u, ROW, [(b, b ^ k) for b in range(G)]) if k else u for k, u in enumerate(updates)]
+    tail, update = call(
+        join_kernel, [shape((32, 40, 128), BF16), shape((G, 256, 128), BF16)], tail, *updates
+    )
+    (update,) = call(update_kernel, [shape((RES * 128, Z), F32)], update)
     tail = exchange(tail, NEAR)
     gl, gr, gout = call(
         final_kernel,

time: 105 us -> 103 us (0.981)
  blocking collectives: 65.5 us -> 45.6 us
  starting transfers between devices: 18.9 us -> 33.6 us
  waiting for transfers between devices: 7.31 us -> 10.4 us
    all_to_all x4 -> x3, blocking collectives: 65.5 us -> 45.6 us  [exchange(): return lax.all_to_all(x, axes, split_axis=0, concat_axis=0, tiled=True)]
    ppermute x0 -> x3, starting transfers between devices: none -> 8.37 us  [per_device(): lax.ppermute(u, ROW, [(b, b ^ k) for b in range(G)])]
    all_to_all x2 -> x3, starting transfers between devices: 13.2 us -> 19.6 us  [exchange(): return lax.all_to_all(x, axes, split_axis=0, concat_axis=0, tiled=True)]
    ppermute x0 -> x3, waiting for transfers between devices: none -> 2.9 us  [per_device(): lax.ppermute(u, ROW, [(b, b ^ k) for b in range(G)])]
    all_to_all x2 -> x3, waiting for transfers between devices: 6.17 us -> 6.38 us  [exchange(): return lax.all_to_all(x, axes, split_axis=0, concat_axis=0, tiled=True)]
  transfers between devices with their start and end apart: 3 -> 7, of which waited for: 2 -> 4; matrix products, arithmetic and copies ran while one was open for 1% -> 1% of each run, Pallas kernels for 1% -> 1%
where the time goes in v5:
time: 103 us; the launch traced here: 102 us
  blocking collectives  45.6 us (44%)
  starting transfers between devices  33.6 us (33%)
  Pallas kernels  11 us (11%)
  waiting for transfers between devices  10.4 us (10%)
  local copies, waits for them, and re-layouts  1.1 us (1%)
    all_to_all x3, blocking collectives, exchange(): return lax.all_to_all(x, axes, split_axis=0, concat_axis=0, tiled=True)  45.6 us
    all_to_all x3, starting transfers between devices, exchange(): return lax.all_to_all(x, axes, split_axis=0, concat_axis=0, tiled=True)  19.6 us
    pallas_call x10, Pallas kernels, call(): pl.pallas_call(kernel, out_shape=out, in_specs=[pl.BlockSpec(memory_space...  11 us
    ppermute x3, starting transfers between devices, per_device(): lax.ppermute(u, ROW, [(b, b ^ k) for b in range(G)])  8.37 us
    all_to_all x3, waiting for transfers between devices, exchange(): return lax.all_to_all(x, axes, split_axis=0, concat_axis=0, tiled=True)  6.38 us
    ppermute x1, starting transfers between devices, per_device(): other = lax.ppermute(gout, 'core', [(0, 1), (1, 0)])  5.61 us
    ppermute x3, waiting for transfers between devices, per_device(): lax.ppermute(u, ROW, [(b, b ^ k) for b in range(G)])  2.9 us
  transfers between devices with their start and end apart: 7, of which 4 were waited for; matrix products, arithmetic and copies ran while one was open for 1% of the time, Pallas kernels for 1%

profile of v5, /device:TPU:1, one launch (start us, length us, event | category | flops | bytes accessed | tf_op | source)
XLA Modules:
  0.0 102.4 jit_solution(16311249284867129721)
XLA Ops:
  0.7 1.3 %shard_map.92 = (bf16[4,512,128]{2,1,0:T(8,128)(2,1)S(1)}, bf16[8,128,256]{2,1,0:T(8,128)(2,1)S(1)}) custom-call(bf16[1024,256]{1,0:T(8,128)(2,1)} %bitcast.16, f32[1024,128]{1,0:T(8,128)} %bitcast.17), custom_call_target="tpu_custom_call" | custom-call | flops 2000000000 | bytes 2097152 | tf_op jit(solution)/shard_map/pallas_call | solution.py:46
  2.0 0.5 shard_map.93
  2.5 11.0 %all_to_all.30.row_ref = bf16[4,512,128]{2,1,0:T(8,128)(2,1)S(1)} all-to-all(bf16[4,512,128]{2,1,0:T(8,128)(2,1)S(1)} %get-tuple-element.30), channel_id=1, replica_groups=mesh['yh'=4,'x'=4,'core'=2,'zh'=4,'zl'=2,'yl'=2] {'zl','yl'}, dimensions={0} | all-to-all | bytes 1048576 | tf_op jit(solution)/shard_map/all_to_all | solution.py:63
  13.5 2.6 %shard_map.94 = (bf16[4,512,128]{2,1,0:T(8,128)(2,1)S(1)}, bf16[1024,1024]{1,0:T(8,128)(2,1)S(1)}, bf16[128,1024]{1,0:T(8,128)(2,1)S(1)}) custom-call(bf16[4,512,128]{2,1,0:T(8,128)(2,1)S(1)} %all_to_all.30.row_ref, bf16[256,128]{1,0:T(8,128)(2,1)S(1)} %get-tuple-element.31.right_ref, bf16[1024,128]{1,0:T(8,128)(2,1)S(1)} %copy-done.2), custom_call_target="tpu_custom_call" | custom-call | flops 536870912 | bytes 3735552 | tf_op jit(solution)/shard_map/pallas_call | solution.py:46
  16.1 22.2 %all_to_all.31.col_ref = bf16[4,512,128]{2,1,0:T(8,128)(2,1)S(1)} all-to-all(bf16[4,512,128]{2,1,0:T(8,128)(2,1)S(1)} %get-tuple-element.32), channel_id=1, replica_groups=mesh['yh'=4,'x'=4,'core'=2,'zh'=4,'zl'=2,'yl'=2] {'zh'}, dimensions={0} | all-to-all | bytes 1048576 | tf_op jit(solution)/shard_map/all_to_all | solution.py:63
  38.3 2.3 %shard_map.95 = (bf16[4,256,128]{2,1,0:T(8,128)(2,1)}, bf16[4,256,128]{2,1,0:T(8,128)(2,1)S(1)}, bf16[1024,128]{1,0:T(8,128)(2,1)S(1)}) custom-call(bf16[4,512,128]{2,1,0:T(8,128)(2,1)S(1)} %all_to_all.30.row_ref, bf16[4,512,128]{2,1,0:T(8,128)(2,1)S(1)} %all_to_all.31.col_ref, bf16[1024,1024]{1,0:T(8,128)(2,1)S(1)} %get-tuple-element.33.grads_ref, ...), custom_call_target="tpu_custom_call" | custom-call | flops 1073741824 | bytes 4194304 | tf_op jit(solution)/shard_map/pallas_call | solution.py:46
  40.6 5.6 %all-to-all-start.2 = ((bf16[4,256,128]{2,1,0:T(8,128)(2,1)}), bf16[4,256,128]{2,1,0:T(8,128)(2,1)S(1)}, u32[]{:S(2)}, u32[]{:S(2)}) async-start(bf16[4,256,128]{2,1,0:T(8,128)(2,1)} %get-tuple-element.35), calls=%async_computation.2 | async-start | bytes 524288 | tf_op jit(solution)/shard_map/all_to_all | solution.py:63
  46.2 5.6 %collective-permute-start = (bf16[1024,128]{1,0:T(8,128)(2,1)S(1)}, bf16[1024,128]{1,0:T(8,128)(2,1)S(1)}, u32[]{:S(2)}, u32[]{:S(2)}) collective-permute-start(bf16[1024,128]{1,0:T(8,128)(2,1)S(1)} %get-tuple-element.36.gout_ref), channel_id=1, source_target_pairs={{0,16},{16,0},{1,17},{17,1},{2,18},{18,2},{3,19},{19,3},{4,20},{20... | collective-permute-start | bytes 786440 | tf_op jit(solution)/shard_map/ppermute | solution.py:294
  51.8 1.1 %collective-permute-done.other_ref = bf16[1024,128]{1,0:T(8,128)(2,1)S(1)} collective-permute-done((bf16[1024,128]{1,0:T(8,128)(2,1)S(1)}, bf16[1024,128]{1,0:T(8,128)(2,1)S(1)}, u32[]{:S(2)}, u32[]{:S(2)}) %collective-permute-start) | collective-permute-done | bytes 262176 | tf_op jit(solution)/shard_map/ppermute | solution.py:294
  53.0 0.4 shard_map.96
  53.4 12.4 %all_to_all.32.in_ref = bf16[16,40,128]{2,1,0:T(8,128)(2,1)S(1)} all-to-all(bf16[16,40,128]{2,1,0:T(8,128)(2,1)S(1)} %get-tuple-element.37), channel_id=1, replica_groups=mesh['yh'=4,'x'=4,'core'=2,'zh'=4,'zl'=2,'yl'=2] {'x','zl','yl'}, dimensions={0} | all-to-all | bytes 327680 | tf_op jit(solution)/shard_map/all_to_all | solution.py:63
  65.8 0.7 shard_map.97
  66.5 6.5 %all-to-all-start.4 = ((bf16[16,40,128]{2,1,0:T(8,128)(2,1)}), bf16[16,40,128]{2,1,0:T(8,128)(2,1)S(1)}, u32[]{:S(2)}, u32[]{:S(2)}) async-start(bf16[16,40,128]{2,1,0:T(8,128)(2,1)} %get-tuple-element.39), calls=%async_computation.4 | async-start | bytes 327680 | tf_op jit(solution)/shard_map/all_to_all | solution.py:63
  73.0 2.6 %collective-permute-start.1 = (bf16[256,128]{1,0:T(8,128)(2,1)S(1)}, bf16[256,128]{1,0:T(8,128)(2,1)S(1)}, u32[]{:S(2)}, u32[]{:S(2)}) collective-permute-start(bf16[256,128]{1,0:T(8,128)(2,1)S(1)} %get-tuple-element.41), channel_id=1, source_target_pairs={{0,1},{1,0},{2,3},{3,2},{4,5},{5,4},{6,7},{7,6},{8,9},{9,8},{10,11... | collective-permute-start | bytes 196616 | tf_op jit(solution)/shard_map/ppermute | solution.py:312
  75.7 2.4 %collective-permute-start.2 = (bf16[256,128]{1,0:T(8,128)(2,1)S(1)}, bf16[256,128]{1,0:T(8,128)(2,1)S(1)}, u32[]{:S(2)}, u32[]{:S(2)}) collective-permute-start(bf16[256,128]{1,0:T(8,128)(2,1)S(1)} %get-tuple-element.42), channel_id=1, source_target_pairs={{0,2},{1,3},{2,0},{3,1},{4,6},{5,7},{6,4},{7,5},{8,10},{9,11},{10,... | collective-permute-start | bytes 196616 | tf_op jit(solution)/shard_map/ppermute | solution.py:312
  78.1 3.3 %collective-permute-start.3 = (bf16[256,128]{1,0:T(8,128)(2,1)S(1)}, bf16[256,128]{1,0:T(8,128)(2,1)S(1)}, u32[]{:S(2)}, u32[]{:S(2)}) collective-permute-start(bf16[256,128]{1,0:T(8,128)(2,1)S(1)} %get-tuple-element.43), channel_id=1, source_target_pairs={{0,3},{1,2},{2,1},{3,0},{4,7},{5,6},{6,5},{7,4},{8,11},{9,10},{10,... | collective-permute-start | bytes 196616 | tf_op jit(solution)/shard_map/ppermute | solution.py:312
  81.5 2.9 %collective-permute-done.3.refs_3_ = bf16[256,128]{1,0:T(8,128)(2,1)S(1)} collective-permute-done((bf16[256,128]{1,0:T(8,128)(2,1)S(1)}, bf16[256,128]{1,0:T(8,128)(2,1)S(1)}, u32[]{:S(2)}, u32[]{:S(2)}) %collective-permute-start.3) | collective-permute-done | bytes 65568 | tf_op jit(solution)/shard_map/ppermute | solution.py:312
  84.7 0.8 shard_map.98
  85.4 7.5 %all-to-all-start.5 = ((bf16[32,40,128]{2,1,0:T(8,128)(2,1)}), bf16[32,40,128]{2,1,0:T(8,128)(2,1)S(1)}, u32[]{:S(2)}, u32[]{:S(2)}) async-start(bf16[32,40,128]{2,1,0:T(8,128)(2,1)} %get-tuple-element.47), calls=%async_computation.5 | async-start | bytes 655360 | tf_op jit(solution)/shard_map/all_to_all | solution.py:63
  92.9 0.3 shard_map.100
  93.2 1.1 %copy.11 = bf16[1,128,8,256]{3,2,1,0:T(8,128)(2,1)} copy(bf16[1,128,8,256]{3,1,2,0:T(8,128)(2,1)S(1)} %bitcast.10) | data formatting | bytes 1048576
  94.3 0.9 shard_map.99
  95.2 6.1 %all-to-all-done.5.in_ref = bf16[32,40,128]{2,1,0:T(8,128)(2,1)S(1)} async-done(((bf16[32,40,128]{2,1,0:T(8,128)(2,1)}), bf16[32,40,128]{2,1,0:T(8,128)(2,1)S(1)}, u32[]{:S(2)}, u32[]{:S(2)}) %all-to-all-start.5) | async-done | bytes 327712 | tf_op jit(solution)/shard_map/all_to_all | solution.py:63
  101.3 1.1 %shard_map.101 = (f32[32,256]{1,0:T(8,128)}, f32[32,256]{1,0:T(8,128)}, f32[1024,128]{1,0:T(8,128)}) custom-call(bf16[32,40,128]{2,1,0:T(8,128)(2,1)S(1)} %all-to-all-done.5.in_ref), custom_call_target="tpu_custom_call" | custom-call | bytes 917504 | tf_op jit(solution)/shard_map/pallas_call | solution.py:46
  (10 shorter events, 0.3 us)
Async XLA Ops:
  0.6 1.3 %copy-start = (bf16[256,32]{0,1:T(8,128)(2,1)S(1)}, bf16[256,32]{0,1:T(8,128)(2,1)}, u32[]{:S(2)}) copy-start(bf16[256,32]{0,1:T(8,128)(2,1)} %param.6) | copy-start | bytes 49156
  0.6 1.3 %copy-start.1 = (bf16[256,32]{0,1:T(8,128)(2,1)S(1)}, bf16[256,32]{0,1:T(8,128)(2,1)}, u32[]{:S(2)}) copy-start(bf16[256,32]{0,1:T(8,128)(2,1)} %param.7) | copy-start | bytes 49156
  2.0 11.5 %copy-start.2 = (bf16[1024,128]{1,0:T(8,128)(2,1)S(1)}, bf16[1024,128]{1,0:T(8,128)(2,1)}, u32[]{:S(2)}) copy-start(bf16[1024,128]{1,0:T(8,128)(2,1)} %w_ref.1) | copy-start | bytes 786436
  40.6 12.3 %all-to-all-start.2 = ((bf16[4,256,128]{2,1,0:T(8,128)(2,1)}), bf16[4,256,128]{2,1,0:T(8,128)(2,1)S(1)}, u32[]{:S(2)}, u32[]{:S(2)}) async-start(bf16[4,256,128]{2,1,0:T(8,128)(2,1)} %get-tuple-element.35), calls=%async_computation.2 | async-start | bytes 524288 | tf_op jit(solution)/shard_map/all_to_all | solution.py:63
  46.2 6.8 %collective-permute-start = (bf16[1024,128]{1,0:T(8,128)(2,1)S(1)}, bf16[1024,128]{1,0:T(8,128)(2,1)S(1)}, u32[]{:S(2)}, u32[]{:S(2)}) collective-permute-start(bf16[1024,128]{1,0:T(8,128)(2,1)S(1)} %get-tuple-element.36.gout_ref), channel_id=1, source_target_pairs={{0,16},{16,0},{1,17},{17,1},{2,18},{18,2},{3,19},{19,3},{4,20},{20... | collective-permute-start | bytes 786440 | tf_op jit(solution)/shard_map/ppermute | solution.py:294
  66.5 18.2 %all-to-all-start.4 = ((bf16[16,40,128]{2,1,0:T(8,128)(2,1)}), bf16[16,40,128]{2,1,0:T(8,128)(2,1)S(1)}, u32[]{:S(2)}, u32[]{:S(2)}) async-start(bf16[16,40,128]{2,1,0:T(8,128)(2,1)} %get-tuple-element.39), calls=%async_computation.4 | async-start | bytes 327680 | tf_op jit(solution)/shard_map/all_to_all | solution.py:63
  73.0 8.4 %collective-permute-start.1 = (bf16[256,128]{1,0:T(8,128)(2,1)S(1)}, bf16[256,128]{1,0:T(8,128)(2,1)S(1)}, u32[]{:S(2)}, u32[]{:S(2)}) collective-permute-start(bf16[256,128]{1,0:T(8,128)(2,1)S(1)} %get-tuple-element.41), channel_id=1, source_target_pairs={{0,1},{1,0},{2,3},{3,2},{4,5},{5,4},{6,7},{7,6},{8,9},{9,8},{10,11... | collective-permute-start | bytes 196616 | tf_op jit(solution)/shard_map/ppermute | solution.py:312
  75.7 5.8 %collective-permute-start.2 = (bf16[256,128]{1,0:T(8,128)(2,1)S(1)}, bf16[256,128]{1,0:T(8,128)(2,1)S(1)}, u32[]{:S(2)}, u32[]{:S(2)}) collective-permute-start(bf16[256,128]{1,0:T(8,128)(2,1)S(1)} %get-tuple-element.42), channel_id=1, source_target_pairs={{0,2},{1,3},{2,0},{3,1},{4,6},{5,7},{6,4},{7,5},{8,10},{9,11},{10,... | collective-permute-start | bytes 196616 | tf_op jit(solution)/shard_map/ppermute | solution.py:312
  78.1 6.2 %collective-permute-start.3 = (bf16[256,128]{1,0:T(8,128)(2,1)S(1)}, bf16[256,128]{1,0:T(8,128)(2,1)S(1)}, u32[]{:S(2)}, u32[]{:S(2)}) collective-permute-start(bf16[256,128]{1,0:T(8,128)(2,1)S(1)} %get-tuple-element.43), channel_id=1, source_target_pairs={{0,3},{1,2},{2,1},{3,0},{4,7},{5,6},{6,5},{7,4},{8,11},{9,10},{10,... | collective-permute-start | bytes 196616 | tf_op jit(solution)/shard_map/ppermute | solution.py:312
  85.4 15.8 %all-to-all-start.5 = ((bf16[32,40,128]{2,1,0:T(8,128)(2,1)}), bf16[32,40,128]{2,1,0:T(8,128)(2,1)S(1)}, u32[]{:S(2)}, u32[]{:S(2)}) async-start(bf16[32,40,128]{2,1,0:T(8,128)(2,1)} %get-tuple-element.47), calls=%async_computation.5 | async-start | bytes 655360 | tf_op jit(solution)/shard_map/all_to_all | solution.py:63

commit v6 on v5

--- a/solution.py
+++ b/solution.py
@@ -126,7 +126,7 @@
 
 
 def right_kernel(row_ref, right_ref, w_ref, col_ref, grads_ref, weight_ref, wide):
-    wide[...] = w_ref[...].astype(F32)
+    wide[0:1024, :] = w_ref[...].astype(F32)
     weight = jnp.concatenate([wide[pl.ds(e, 32, stride=32), :] for e in range(C)], axis=0)
     weight_ref[...] = weight.T.astype(BF16)
     weight = weight.astype(BF16)
@@ -178,7 +178,8 @@
     half = pl.ds(pl.multiple_of(lax.axis_index("core") * 512, 512), 512)
     gout = gout_ref[half, :].astype(F32) + other_ref[half, :].astype(F32)
     for k in range(16):
-        tail_ref[k] = jnp.concatenate([gout[k * 32 : k * 32 + 32], rows[k * 8 : k * 8 + 8]], axis=0).astype(BF16)
+        block = [gout[k * 32 : k * 32 + 32], rows[k * 8 : k * 8 + 8], jnp.zeros((8, 128), F32)]
+        tail_ref[k] = jnp.concatenate(block, axis=0).astype(BF16)
 
 
 def place():
@@ -253,7 +254,7 @@
         scratch=[
             pltpu.VMEM((S * RES, F), BF16),
             pltpu.VMEM((RES * 128, Z), F32),
-            pltpu.VMEM((2, S * RES, 128), F32),
+            pltpu.VMEM((2, S * RES + 8, 128), F32),
             pltpu.SemaphoreType.DMA((4,)),
         ],
         hbm=True,
@@ -277,7 +278,7 @@
         row,
         right,
         w,
-        scratch=[pltpu.VMEM((1024, 128), F32)],
+        scratch=[pltpu.VMEM((1056, 128), F32)],
         flops=2 * 2 * 1024 * 1024 * 128,
     )
     col = exchange(col, COL)
@@ -295,7 +296,7 @@
     back = exchange(back, ROW)
     left, right, tail = call(
         factor_kernel,
-        [shape((256, S), BF16), shape((256, S), BF16), shape((16, 40, 128), BF16)],
+        [shape((256, S), BF16), shape((256, S), BF16), shape((16, 48, 128), BF16)],
         back,
         col,
         x,
@@ -306,12 +307,12 @@
     (msa,) = call(msa_kernel, [shape((RES, S, F), BF16)], left, right, f1, f2, flops=33554432)
     tail = exchange(tail, NEAREST)
     tail, *updates = call(
-        split_kernel, [shape((16, 40, 128), BF16)] + [shape((256, 128), BF16)] * G, tail, update
+        split_kernel, [shape((16, 48, 128), BF16)] + [shape((256, 128), BF16)] * G, tail, update
     )
     tail = exchange(tail, FAR)
     updates = [lax.ppermute(u, ROW, [(b, b ^ k) for b in range(G)]) if k else u for k, u in enumerate(updates)]
     tail, update = call(
-        join_kernel, [shape((32, 40, 128), BF16), shape((G, 256, 128), BF16)], tail, *updates
+        join_kernel, [shape((32, 48, 128), BF16), shape((G, 256, 128), BF16)], tail, *updates
     )
     (update,) = call(update_kernel, [shape((RES * 128, Z), F32)], update)
     tail = exchange(tail, NEAR)
@@ -319,7 +320,7 @@
         final_kernel,
         [shape((C, F), F32), shape((C, F), F32), shape((1024, 128), F32)],
         tail,
-        scratch=[pltpu.VMEM((1024, 128), F32)],
+        scratch=[pltpu.VMEM((1056, 128), F32)],
     )
     return update.reshape(1, RES, 128, Z), msa.transpose(1, 0, 2)[None], gl.T, gr.T, gout
 

time: 103 us -> 104 us (level)
  transfers between devices with their start and end apart: 7 -> 7, of which waited for: 4 -> 5; matrix products, arithmetic and copies ran while one was open for 1% -> 1% of each run, Pallas kernels for 1% -> 1%
where the time goes in v6:
time: 104 us; the launch traced here: 103 us
  blocking collectives  45.7 us (44%)
  starting transfers between devices  33.5 us (32%)
  waiting for transfers between devices  11.2 us (11%)
  Pallas kernels  11 us (11%)
  local copies, waits for them, and re-layouts  1.1 us (1%)
    all_to_all x3, blocking collectives, exchange(): return lax.all_to_all(x, axes, split_axis=0, concat_axis=0, tiled=True)  45.7 us
    all_to_all x3, starting transfers between devices, exchange(): return lax.all_to_all(x, axes, split_axis=0, concat_axis=0, tiled=True)  19.5 us
    pallas_call x10, Pallas kernels, call(): pl.pallas_call(kernel, out_shape=out, in_specs=[pl.BlockSpec(memory_space...  11 us
    ppermute x3, starting transfers between devices, per_device(): lax.ppermute(u, ROW, [(b, b ^ k) for b in range(G)])  8.37 us
    all_to_all x3, waiting for transfers between devices, exchange(): return lax.all_to_all(x, axes, split_axis=0, concat_axis=0, tiled=True)  6.88 us
    ppermute x1, starting transfers between devices, per_device(): other = lax.ppermute(gout, 'core', [(0, 1), (1, 0)])  5.61 us
    ppermute x3, waiting for transfers between devices, per_device(): lax.ppermute(u, ROW, [(b, b ^ k) for b in range(G)])  3.19 us
  transfers between devices with their start and end apart: 7, of which 5 were waited for; matrix products, arithmetic and copies ran while one was open for 1% of the time, Pallas kernels for 1%

profile of v6, /device:TPU:1, one launch (start us, length us, event | category | flops | bytes accessed | tf_op | source)
XLA Modules:
  0.0 103.2 jit_solution(9440956766000871252)
XLA Ops:
  0.7 1.3 %shard_map.92 = (bf16[4,512,128]{2,1,0:T(8,128)(2,1)S(1)}, bf16[8,128,256]{2,1,0:T(8,128)(2,1)S(1)}) custom-call(bf16[1024,256]{1,0:T(8,128)(2,1)} %bitcast.16, f32[1024,128]{1,0:T(8,128)} %bitcast.17), custom_call_target="tpu_custom_call" | custom-call | flops 2000000000 | bytes 2097152 | tf_op jit(solution)/shard_map/pallas_call | solution.py:46
  2.0 0.5 shard_map.93
  2.5 11.0 %all_to_all.30.row_ref = bf16[4,512,128]{2,1,0:T(8,128)(2,1)S(1)} all-to-all(bf16[4,512,128]{2,1,0:T(8,128)(2,1)S(1)} %get-tuple-element.30), channel_id=1, replica_groups=mesh['yh'=4,'x'=4,'core'=2,'zh'=4,'zl'=2,'yl'=2] {'zl','yl'}, dimensions={0} | all-to-all | bytes 1048576 | tf_op jit(solution)/shard_map/all_to_all | solution.py:63
  13.5 2.6 %shard_map.94 = (bf16[4,512,128]{2,1,0:T(8,128)(2,1)S(1)}, bf16[1024,1024]{1,0:T(8,128)(2,1)S(1)}, bf16[128,1024]{1,0:T(8,128)(2,1)S(1)}) custom-call(bf16[4,512,128]{2,1,0:T(8,128)(2,1)S(1)} %all_to_all.30.row_ref, bf16[256,128]{1,0:T(8,128)(2,1)S(1)} %get-tuple-element.31.right_ref, bf16[1024,128]{1,0:T(8,128)(2,1)S(1)} %copy-done.2), custom_call_target="tpu_custom_call" | custom-call | flops 536870912 | bytes 3735552 | tf_op jit(solution)/shard_map/pallas_call | solution.py:46
  16.1 22.2 %all_to_all.31.col_ref = bf16[4,512,128]{2,1,0:T(8,128)(2,1)S(1)} all-to-all(bf16[4,512,128]{2,1,0:T(8,128)(2,1)S(1)} %get-tuple-element.32), channel_id=1, replica_groups=mesh['yh'=4,'x'=4,'core'=2,'zh'=4,'zl'=2,'yl'=2] {'zh'}, dimensions={0} | all-to-all | bytes 1048576 | tf_op jit(solution)/shard_map/all_to_all | solution.py:63
  38.3 2.3 %shard_map.95 = (bf16[4,256,128]{2,1,0:T(8,128)(2,1)}, bf16[4,256,128]{2,1,0:T(8,128)(2,1)S(1)}, bf16[1024,128]{1,0:T(8,128)(2,1)S(1)}) custom-call(bf16[4,512,128]{2,1,0:T(8,128)(2,1)S(1)} %all_to_all.30.row_ref, bf16[4,512,128]{2,1,0:T(8,128)(2,1)S(1)} %all_to_all.31.col_ref, bf16[1024,1024]{1,0:T(8,128)(2,1)S(1)} %get-tuple-element.33.grads_ref, ...), custom_call_target="tpu_custom_call" | custom-call | flops 1073741824 | bytes 4194304 | tf_op jit(solution)/shard_map/pallas_call | solution.py:46
  40.6 5.6 %all-to-all-start.2 = ((bf16[4,256,128]{2,1,0:T(8,128)(2,1)}), bf16[4,256,128]{2,1,0:T(8,128)(2,1)S(1)}, u32[]{:S(2)}, u32[]{:S(2)}) async-start(bf16[4,256,128]{2,1,0:T(8,128)(2,1)} %get-tuple-element.35), calls=%async_computation.2 | async-start | bytes 524288 | tf_op jit(solution)/shard_map/all_to_all | solution.py:63
  46.2 5.6 %collective-permute-start = (bf16[1024,128]{1,0:T(8,128)(2,1)S(1)}, bf16[1024,128]{1,0:T(8,128)(2,1)S(1)}, u32[]{:S(2)}, u32[]{:S(2)}) collective-permute-start(bf16[1024,128]{1,0:T(8,128)(2,1)S(1)} %get-tuple-element.36.gout_ref), channel_id=1, source_target_pairs={{0,16},{16,0},{1,17},{17,1},{2,18},{18,2},{3,19},{19,3},{4,20},{20... | collective-permute-start | bytes 786440 | tf_op jit(solution)/shard_map/ppermute | solution.py:295
  51.8 1.1 %collective-permute-done.other_ref = bf16[1024,128]{1,0:T(8,128)(2,1)S(1)} collective-permute-done((bf16[1024,128]{1,0:T(8,128)(2,1)S(1)}, bf16[1024,128]{1,0:T(8,128)(2,1)S(1)}, u32[]{:S(2)}, u32[]{:S(2)}) %collective-permute-start) | collective-permute-done | bytes 262176 | tf_op jit(solution)/shard_map/ppermute | solution.py:295
  53.0 0.4 shard_map.96
  53.4 12.5 %all_to_all.32.in_ref = bf16[16,48,128]{2,1,0:T(8,128)(2,1)S(1)} all-to-all(bf16[16,48,128]{2,1,0:T(8,128)(2,1)S(1)} %get-tuple-element.37), channel_id=1, replica_groups=mesh['yh'=4,'x'=4,'core'=2,'zh'=4,'zl'=2,'yl'=2] {'x','zl','yl'}, dimensions={0} | all-to-all | bytes 393216 | tf_op jit(solution)/shard_map/all_to_all | solution.py:63
  65.9 0.7 shard_map.97
  66.6 6.6 %all-to-all-start.4 = ((bf16[16,48,128]{2,1,0:T(8,128)(2,1)}), bf16[16,48,128]{2,1,0:T(8,128)(2,1)S(1)}, u32[]{:S(2)}, u32[]{:S(2)}) async-start(bf16[16,48,128]{2,1,0:T(8,128)(2,1)} %get-tuple-element.39), calls=%async_computation.4 | async-start | bytes 393216 | tf_op jit(solution)/shard_map/all_to_all | solution.py:63
  73.2 2.7 %collective-permute-start.1 = (bf16[256,128]{1,0:T(8,128)(2,1)S(1)}, bf16[256,128]{1,0:T(8,128)(2,1)S(1)}, u32[]{:S(2)}, u32[]{:S(2)}) collective-permute-start(bf16[256,128]{1,0:T(8,128)(2,1)S(1)} %get-tuple-element.41), channel_id=1, source_target_pairs={{0,1},{1,0},{2,3},{3,2},{4,5},{5,4},{6,7},{7,6},{8,9},{9,8},{10,11... | collective-permute-start | bytes 196616 | tf_op jit(solution)/shard_map/ppermute | solution.py:313
  75.8 2.5 %collective-permute-start.2 = (bf16[256,128]{1,0:T(8,128)(2,1)S(1)}, bf16[256,128]{1,0:T(8,128)(2,1)S(1)}, u32[]{:S(2)}, u32[]{:S(2)}) collective-permute-start(bf16[256,128]{1,0:T(8,128)(2,1)S(1)} %get-tuple-element.42), channel_id=1, source_target_pairs={{0,2},{1,3},{2,0},{3,1},{4,6},{5,7},{6,4},{7,5},{8,10},{9,11},{10,... | collective-permute-start | bytes 196616 | tf_op jit(solution)/shard_map/ppermute | solution.py:313
  78.3 3.2 %collective-permute-start.3 = (bf16[256,128]{1,0:T(8,128)(2,1)S(1)}, bf16[256,128]{1,0:T(8,128)(2,1)S(1)}, u32[]{:S(2)}, u32[]{:S(2)}) collective-permute-start(bf16[256,128]{1,0:T(8,128)(2,1)S(1)} %get-tuple-element.43), channel_id=1, source_target_pairs={{0,3},{1,2},{2,1},{3,0},{4,7},{5,6},{6,5},{7,4},{8,11},{9,10},{10,... | collective-permute-start | bytes 196616 | tf_op jit(solution)/shard_map/ppermute | solution.py:313
  81.7 3.1 %collective-permute-done.3.refs_3_ = bf16[256,128]{1,0:T(8,128)(2,1)S(1)} collective-permute-done((bf16[256,128]{1,0:T(8,128)(2,1)S(1)}, bf16[256,128]{1,0:T(8,128)(2,1)S(1)}, u32[]{:S(2)}, u32[]{:S(2)}) %collective-permute-start.3) | collective-permute-done | bytes 65568 | tf_op jit(solution)/shard_map/ppermute | solution.py:313
  84.9 0.8 shard_map.98
  85.7 7.4 %all-to-all-start.5 = ((bf16[32,48,128]{2,1,0:T(8,128)(2,1)}), bf16[32,48,128]{2,1,0:T(8,128)(2,1)S(1)}, u32[]{:S(2)}, u32[]{:S(2)}) async-start(bf16[32,48,128]{2,1,0:T(8,128)(2,1)} %get-tuple-element.47), calls=%async_computation.5 | async-start | bytes 786432 | tf_op jit(solution)/shard_map/all_to_all | solution.py:63
  93.1 0.3 shard_map.100
  93.5 1.1 %copy.11 = bf16[1,128,8,256]{3,2,1,0:T(8,128)(2,1)} copy(bf16[1,128,8,256]{3,1,2,0:T(8,128)(2,1)S(1)} %bitcast.10) | data formatting | bytes 1048576
  94.5 0.9 shard_map.99
  95.4 6.7 %all-to-all-done.5.in_ref = bf16[32,48,128]{2,1,0:T(8,128)(2,1)S(1)} async-done(((bf16[32,48,128]{2,1,0:T(8,128)(2,1)}), bf16[32,48,128]{2,1,0:T(8,128)(2,1)S(1)}, u32[]{:S(2)}, u32[]{:S(2)}) %all-to-all-start.5) | async-done | bytes 393248 | tf_op jit(solution)/shard_map/all_to_all | solution.py:63
  102.1 1.1 %shard_map.101 = (f32[32,256]{1,0:T(8,128)}, f32[32,256]{1,0:T(8,128)}, f32[1024,128]{1,0:T(8,128)}) custom-call(bf16[32,48,128]{2,1,0:T(8,128)(2,1)S(1)} %all-to-all-done.5.in_ref), custom_call_target="tpu_custom_call" | custom-call | bytes 983040 | tf_op jit(solution)/shard_map/pallas_call | solution.py:46
  (10 shorter events, 0.3 us)
Async XLA Ops:
  0.6 1.3 %copy-start = (bf16[256,32]{0,1:T(8,128)(2,1)S(1)}, bf16[256,32]{0,1:T(8,128)(2,1)}, u32[]{:S(2)}) copy-start(bf16[256,32]{0,1:T(8,128)(2,1)} %param.6) | copy-start | bytes 49156
  0.6 1.3 %copy-start.1 = (bf16[256,32]{0,1:T(8,128)(2,1)S(1)}, bf16[256,32]{0,1:T(8,128)(2,1)}, u32[]{:S(2)}) copy-start(bf16[256,32]{0,1:T(8,128)(2,1)} %param.7) | copy-start | bytes 49156
  2.0 11.5 %copy-start.2 = (bf16[1024,128]{1,0:T(8,128)(2,1)S(1)}, bf16[1024,128]{1,0:T(8,128)(2,1)}, u32[]{:S(2)}) copy-start(bf16[1024,128]{1,0:T(8,128)(2,1)} %w_ref.1) | copy-start | bytes 786436
  40.6 12.3 %all-to-all-start.2 = ((bf16[4,256,128]{2,1,0:T(8,128)(2,1)}), bf16[4,256,128]{2,1,0:T(8,128)(2,1)S(1)}, u32[]{:S(2)}, u32[]{:S(2)}) async-start(bf16[4,256,128]{2,1,0:T(8,128)(2,1)} %get-tuple-element.35), calls=%async_computation.2 | async-start | bytes 524288 | tf_op jit(solution)/shard_map/all_to_all | solution.py:63
  46.2 6.8 %collective-permute-start = (bf16[1024,128]{1,0:T(8,128)(2,1)S(1)}, bf16[1024,128]{1,0:T(8,128)(2,1)S(1)}, u32[]{:S(2)}, u32[]{:S(2)}) collective-permute-start(bf16[1024,128]{1,0:T(8,128)(2,1)S(1)} %get-tuple-element.36.gout_ref), channel_id=1, source_target_pairs={{0,16},{16,0},{1,17},{17,1},{2,18},{18,2},{3,19},{19,3},{4,20},{20... | collective-permute-start | bytes 786440 | tf_op jit(solution)/shard_map/ppermute | solution.py:295
  66.6 18.3 %all-to-all-start.4 = ((bf16[16,48,128]{2,1,0:T(8,128)(2,1)}), bf16[16,48,128]{2,1,0:T(8,128)(2,1)S(1)}, u32[]{:S(2)}, u32[]{:S(2)}) async-start(bf16[16,48,128]{2,1,0:T(8,128)(2,1)} %get-tuple-element.39), calls=%async_computation.4 | async-start | bytes 393216 | tf_op jit(solution)/shard_map/all_to_all | solution.py:63
  73.2 8.4 %collective-permute-start.1 = (bf16[256,128]{1,0:T(8,128)(2,1)S(1)}, bf16[256,128]{1,0:T(8,128)(2,1)S(1)}, u32[]{:S(2)}, u32[]{:S(2)}) collective-permute-start(bf16[256,128]{1,0:T(8,128)(2,1)S(1)} %get-tuple-element.41), channel_id=1, source_target_pairs={{0,1},{1,0},{2,3},{3,2},{4,5},{5,4},{6,7},{7,6},{8,9},{9,8},{10,11... | collective-permute-start | bytes 196616 | tf_op jit(solution)/shard_map/ppermute | solution.py:313
  75.8 5.8 %collective-permute-start.2 = (bf16[256,128]{1,0:T(8,128)(2,1)S(1)}, bf16[256,128]{1,0:T(8,128)(2,1)S(1)}, u32[]{:S(2)}, u32[]{:S(2)}) collective-permute-start(bf16[256,128]{1,0:T(8,128)(2,1)S(1)} %get-tuple-element.42), channel_id=1, source_target_pairs={{0,2},{1,3},{2,0},{3,1},{4,6},{5,7},{6,4},{7,5},{8,10},{9,11},{10,... | collective-permute-start | bytes 196616 | tf_op jit(solution)/shard_map/ppermute | solution.py:313
  78.3 6.4 %collective-permute-start.3 = (bf16[256,128]{1,0:T(8,128)(2,1)S(1)}, bf16[256,128]{1,0:T(8,128)(2,1)S(1)}, u32[]{:S(2)}, u32[]{:S(2)}) collective-permute-start(bf16[256,128]{1,0:T(8,128)(2,1)S(1)} %get-tuple-element.43), channel_id=1, source_target_pairs={{0,3},{1,2},{2,1},{3,0},{4,7},{5,6},{6,5},{7,4},{8,11},{9,10},{10,... | collective-permute-start | bytes 196616 | tf_op jit(solution)/shard_map/ppermute | solution.py:313
  85.7 16.3 %all-to-all-start.5 = ((bf16[32,48,128]{2,1,0:T(8,128)(2,1)}), bf16[32,48,128]{2,1,0:T(8,128)(2,1)S(1)}, u32[]{:S(2)}, u32[]{:S(2)}) async-start(bf16[32,48,128]{2,1,0:T(8,128)(2,1)} %get-tuple-element.47), calls=%async_computation.5 | async-start | bytes 786432 | tf_op jit(solution)/shard_map/all_to_all | solution.py:63

commit v7 on v6

--- a/solution.py
+++ b/solution.py
@@ -57,6 +57,10 @@
 
 def shape(dims, dtype):
     return jax.ShapeDtypeStruct(dims, dtype)
+
+
+def partner(x, k):
+    return lax.ppermute(x, ROW, [(b, b ^ k) for b in range(G)])
 
 
 def exchange(x, axes):
@@ -186,27 +190,31 @@
     return lax.axis_index("zl") * 2 + lax.axis_index("yl")
 
 
-def split_kernel(in_ref, update_ref, out_ref, *part_refs):
+def split_kernel(in_ref, update_ref, out_ref, pair_ref):
     sum_kernel(in_ref, out_ref)
     me = place()
-    for k, ref in enumerate(part_refs):
-        ref[...] = update_ref[lax.bitwise_xor(me, k)]
-
-
-def join_kernel(in_ref, *refs):
-    sum_kernel(in_ref, refs[G])
+    pair_ref[0] = update_ref[lax.bitwise_xor(me, 2)]
+    pair_ref[1] = update_ref[lax.bitwise_xor(me, 3)]
+
+
+def join_kernel(in_ref, update_ref, got_ref, out_ref, own_ref, a_ref, pair_ref):
+    sum_kernel(in_ref, out_ref)
     me = place()
-    for k in range(G):
-        refs[G + 1][lax.bitwise_xor(me, k)] = refs[k][...]
-
-
-def update_kernel(update_ref, out_ref):
-    for b in range(G):
-        part = update_ref[b].astype(F32)
+    own_ref[...] = update_ref[me]
+    a_ref[...] = got_ref[0]
+    pair_ref[0] = update_ref[lax.bitwise_xor(me, 1)]
+    pair_ref[1] = got_ref[1]
+
+
+def update_kernel(own_ref, a_ref, pair_ref, out_ref):
+    me = place()
+    for k, block in enumerate((own_ref[...], pair_ref[0], a_ref[...], pair_ref[1])):
+        b = lax.bitwise_xor(me, k)
+        part = block.astype(F32)
         for i in range(RES):
             for a in range(G):
-                at = i * 128 + a * 32 + b * 8
-                out_ref[at : at + 8, :] = part[i * 32 + a * 8 : i * 32 + a * 8 + 8, :]
+                at = pl.multiple_of(i * 128 + a * 32 + b * 8, 8)
+                out_ref[pl.ds(at, 8), :] = part[i * 32 + a * 8 : i * 32 + a * 8 + 8, :]
 
 
 def msa_kernel(left_ref, right_ref, f1_ref, f2_ref, out_ref):
@@ -306,15 +314,13 @@
     )
     (msa,) = call(msa_kernel, [shape((RES, S, F), BF16)], left, right, f1, f2, flops=33554432)
     tail = exchange(tail, NEAREST)
-    tail, *updates = call(
-        split_kernel, [shape((16, 48, 128), BF16)] + [shape((256, 128), BF16)] * G, tail, update
-    )
+    part, pair = shape((256, 128), BF16), shape((2, 256, 128), BF16)
+    tail, first = call(split_kernel, [shape((16, 48, 128), BF16), pair], tail, update)
     tail = exchange(tail, FAR)
-    updates = [lax.ppermute(u, ROW, [(b, b ^ k) for b in range(G)]) if k else u for k, u in enumerate(updates)]
-    tail, update = call(
-        join_kernel, [shape((32, 48, 128), BF16), shape((G, 256, 128), BF16)], tail, *updates
-    )
-    (update,) = call(update_kernel, [shape((RES * 128, Z), F32)], update)
+    tail, own, near, second = call(
+        join_kernel, [shape((32, 48, 128), BF16), part, part, pair], tail, update, partner(first, 2)
+    )
+    (update,) = call(update_kernel, [shape((RES * 128, Z), F32)], own, near, partner(second, 1))
     tail = exchange(tail, NEAR)
     gl, gr, gout = call(
         final_kernel,

time: 104 us -> 105 us (level)
  waiting for transfers between devices: 11.2 us -> 14.9 us
  starting transfers between devices: 33.5 us -> 30.7 us
    ppermute x3 -> x2, waiting for transfers between devices: 3.19 us -> 8.83 us  [partner(): return lax.ppermute(x, ROW, [(b, b ^ k) for b in range(G)])]
    ppermute x3 -> x2, starting transfers between devices: 8.37 us -> 5.85 us  [partner(): return lax.ppermute(x, ROW, [(b, b ^ k) for b in range(G)])]
    all_to_all x3, waiting for transfers between devices: 6.88 us -> 4.89 us  [exchange(): return lax.all_to_all(x, axes, split_axis=0, concat_axis=0, tiled=True)]
  transfers between devices with their start and end apart: 7 -> 6, of which waited for: 5 -> 4; matrix products, arithmetic and copies ran while one was open for 1% -> 1% of each run, Pallas kernels for 1% -> 1%
where the time goes in v7:
time: 105 us; the launch traced here: 104 us
  blocking collectives  45.7 us (44%)
  starting transfers between devices  30.7 us (29%)
  waiting for transfers between devices  14.9 us (14%)
  Pallas kernels  11 us (10%)
  local copies, waits for them, and re-layouts  1.1 us (1%)
    all_to_all x3, blocking collectives, exchange(): return lax.all_to_all(x, axes, split_axis=0, concat_axis=0, tiled=True)  45.7 us
    all_to_all x3, starting transfers between devices, exchange(): return lax.all_to_all(x, axes, split_axis=0, concat_axis=0, tiled=True)  19.3 us
    pallas_call x10, Pallas kernels, call(): pl.pallas_call(kernel, out_shape=out, in_specs=[pl.BlockSpec(memory_space...  11 us
    ppermute x2, waiting for transfers between devices, partner(): return lax.ppermute(x, ROW, [(b, b ^ k) for b in range(G)])  8.83 us
    ppermute x2, starting transfers between devices, partner(): return lax.ppermute(x, ROW, [(b, b ^ k) for b in range(G)])  5.85 us
    ppermute x1, starting transfers between devices, per_device(): other = lax.ppermute(gout, 'core', [(0, 1), (1, 0)])  5.61 us
    all_to_all x3, waiting for transfers between devices, exchange(): return lax.all_to_all(x, axes, split_axis=0, concat_axis=0, tiled=True)  4.89 us
  transfers between devices with their start and end apart: 6, of which 4 were waited for; matrix products, arithmetic and copies ran while one was open for 1% of the time, Pallas kernels for 1%

profile of v7, /device:TPU:1, one launch (start us, length us, event | category | flops | bytes accessed | tf_op | source)
XLA Modules:
  0.0 104.1 jit_solution(1056983827287644303)
XLA Ops:
  0.7 1.3 %shard_map.92 = (bf16[4,512,128]{2,1,0:T(8,128)(2,1)S(1)}, bf16[8,128,256]{2,1,0:T(8,128)(2,1)S(1)}) custom-call(bf16[1024,256]{1,0:T(8,128)(2,1)} %bitcast.16, f32[1024,128]{1,0:T(8,128)} %bitcast.17), custom_call_target="tpu_custom_call" | custom-call | flops 2000000000 | bytes 2097152 | tf_op jit(solution)/shard_map/pallas_call | solution.py:46
  2.0 0.5 shard_map.93
  2.5 11.0 %all_to_all.30.row_ref = bf16[4,512,128]{2,1,0:T(8,128)(2,1)S(1)} all-to-all(bf16[4,512,128]{2,1,0:T(8,128)(2,1)S(1)} %get-tuple-element.29), channel_id=1, replica_groups=mesh['yh'=4,'x'=4,'core'=2,'zh'=4,'zl'=2,'yl'=2] {'zl','yl'}, dimensions={0} | all-to-all | bytes 1048576 | tf_op jit(solution)/shard_map/all_to_all | solution.py:67
  13.5 2.6 %shard_map.94 = (bf16[4,512,128]{2,1,0:T(8,128)(2,1)S(1)}, bf16[1024,1024]{1,0:T(8,128)(2,1)S(1)}, bf16[128,1024]{1,0:T(8,128)(2,1)S(1)}) custom-call(bf16[4,512,128]{2,1,0:T(8,128)(2,1)S(1)} %all_to_all.30.row_ref, bf16[256,128]{1,0:T(8,128)(2,1)S(1)} %get-tuple-element.30.right_ref, bf16[1024,128]{1,0:T(8,128)(2,1)S(1)} %copy-done.2), custom_call_target="tpu_custom_call" | custom-call | flops 536870912 | bytes 3735552 | tf_op jit(solution)/shard_map/pallas_call | solution.py:46
  16.1 22.2 %all_to_all.31.col_ref = bf16[4,512,128]{2,1,0:T(8,128)(2,1)S(1)} all-to-all(bf16[4,512,128]{2,1,0:T(8,128)(2,1)S(1)} %get-tuple-element.31), channel_id=1, replica_groups=mesh['yh'=4,'x'=4,'core'=2,'zh'=4,'zl'=2,'yl'=2] {'zh'}, dimensions={0} | all-to-all | bytes 1048576 | tf_op jit(solution)/shard_map/all_to_all | solution.py:67
  38.3 2.3 %shard_map.95 = (bf16[4,256,128]{2,1,0:T(8,128)(2,1)}, bf16[4,256,128]{2,1,0:T(8,128)(2,1)S(1)}, bf16[1024,128]{1,0:T(8,128)(2,1)S(1)}) custom-call(bf16[4,512,128]{2,1,0:T(8,128)(2,1)S(1)} %all_to_all.30.row_ref, bf16[4,512,128]{2,1,0:T(8,128)(2,1)S(1)} %all_to_all.31.col_ref, bf16[1024,1024]{1,0:T(8,128)(2,1)S(1)} %get-tuple-element.32.grads_ref, ...), custom_call_target="tpu_custom_call" | custom-call | flops 1073741824 | bytes 4194304 | tf_op jit(solution)/shard_map/pallas_call | solution.py:46
  40.6 5.6 %all-to-all-start.2 = ((bf16[4,256,128]{2,1,0:T(8,128)(2,1)}), bf16[4,256,128]{2,1,0:T(8,128)(2,1)S(1)}, u32[]{:S(2)}, u32[]{:S(2)}) async-start(bf16[4,256,128]{2,1,0:T(8,128)(2,1)} %get-tuple-element.34), calls=%async_computation.2 | async-start | bytes 524288 | tf_op jit(solution)/shard_map/all_to_all | solution.py:67
  46.2 5.6 %collective-permute-start = (bf16[1024,128]{1,0:T(8,128)(2,1)S(1)}, bf16[1024,128]{1,0:T(8,128)(2,1)S(1)}, u32[]{:S(2)}, u32[]{:S(2)}) collective-permute-start(bf16[1024,128]{1,0:T(8,128)(2,1)S(1)} %get-tuple-element.35.gout_ref), channel_id=1, source_target_pairs={{0,16},{16,0},{1,17},{17,1},{2,18},{18,2},{3,19},{19,3},{4,20},{20... | collective-permute-start | bytes 786440 | tf_op jit(solution)/shard_map/ppermute | solution.py:303
  51.8 1.1 %collective-permute-done.other_ref = bf16[1024,128]{1,0:T(8,128)(2,1)S(1)} collective-permute-done((bf16[1024,128]{1,0:T(8,128)(2,1)S(1)}, bf16[1024,128]{1,0:T(8,128)(2,1)S(1)}, u32[]{:S(2)}, u32[]{:S(2)}) %collective-permute-start) | collective-permute-done | bytes 262176 | tf_op jit(solution)/shard_map/ppermute | solution.py:303
  53.0 0.4 shard_map.96
  53.4 12.5 %all_to_all.32.in_ref = bf16[16,48,128]{2,1,0:T(8,128)(2,1)S(1)} all-to-all(bf16[16,48,128]{2,1,0:T(8,128)(2,1)S(1)} %get-tuple-element.36), channel_id=1, replica_groups=mesh['yh'=4,'x'=4,'core'=2,'zh'=4,'zl'=2,'yl'=2] {'x','zl','yl'}, dimensions={0} | all-to-all | bytes 393216 | tf_op jit(solution)/shard_map/all_to_all | solution.py:67
  65.9 0.7 shard_map.97
  66.6 6.6 %all-to-all-start.4 = ((bf16[16,48,128]{2,1,0:T(8,128)(2,1)}), bf16[16,48,128]{2,1,0:T(8,128)(2,1)S(1)}, u32[]{:S(2)}, u32[]{:S(2)}) async-start(bf16[16,48,128]{2,1,0:T(8,128)(2,1)} %get-tuple-element.38), calls=%async_computation.4 | async-start | bytes 393216 | tf_op jit(solution)/shard_map/all_to_all | solution.py:67
  73.2 2.6 %collective-permute-start.1 = (bf16[2,256,128]{2,1,0:T(8,128)(2,1)S(1)}, bf16[2,256,128]{2,1,0:T(8,128)(2,1)S(1)}, u32[]{:S(2)}, u32[]{:S(2)}) collective-permute-start(bf16[2,256,128]{2,1,0:T(8,128)(2,1)S(1)} %get-tuple-element.39), channel_id=1, source_target_pairs={{0,2},{1,3},{2,0},{3,1},{4,6},{5,7},{6,4},{7,5},{8,10},{9,11},{10,... | collective-permute-start | bytes 393224 | tf_op jit(solution)/shard_map/ppermute | solution.py:63
  75.7 4.3 %collective-permute-done.1.got_ref = bf16[2,256,128]{2,1,0:T(8,128)(2,1)S(1)} collective-permute-done((bf16[2,256,128]{2,1,0:T(8,128)(2,1)S(1)}, bf16[2,256,128]{2,1,0:T(8,128)(2,1)S(1)}, u32[]{:S(2)}, u32[]{:S(2)}) %collective-permute-start.1) | collective-permute-done | bytes 131104 | tf_op jit(solution)/shard_map/ppermute | solution.py:63
  80.0 4.9 %all-to-all-done.4.in_ref = bf16[16,48,128]{2,1,0:T(8,128)(2,1)S(1)} async-done(((bf16[16,48,128]{2,1,0:T(8,128)(2,1)}), bf16[16,48,128]{2,1,0:T(8,128)(2,1)S(1)}, u32[]{:S(2)}, u32[]{:S(2)}) %all-to-all-start.4) | async-done | bytes 196640 | tf_op jit(solution)/shard_map/all_to_all | solution.py:67
  84.9 0.8 shard_map.98
  85.7 7.2 %all-to-all-start.5 = ((bf16[32,48,128]{2,1,0:T(8,128)(2,1)}), bf16[32,48,128]{2,1,0:T(8,128)(2,1)S(1)}, u32[]{:S(2)}, u32[]{:S(2)}) async-start(bf16[32,48,128]{2,1,0:T(8,128)(2,1)} %get-tuple-element.45), calls=%async_computation.5 | async-start | bytes 786432 | tf_op jit(solution)/shard_map/all_to_all | solution.py:67
  92.8 3.3 %collective-permute-start.2 = (bf16[2,256,128]{2,1,0:T(8,128)(2,1)S(1)}, bf16[2,256,128]{2,1,0:T(8,128)(2,1)S(1)}, u32[]{:S(2)}, u32[]{:S(2)}) collective-permute-start(bf16[2,256,128]{2,1,0:T(8,128)(2,1)S(1)} %get-tuple-element.42), channel_id=1, source_target_pairs={{0,1},{1,0},{2,3},{3,2},{4,5},{5,4},{6,7},{7,6},{8,9},{9,8},{10,11... | collective-permute-start | bytes 393224 | tf_op jit(solution)/shard_map/ppermute | solution.py:63
  96.1 0.3 shard_map.100
  96.5 1.1 %copy.11 = bf16[1,128,8,256]{3,2,1,0:T(8,128)(2,1)} copy(bf16[1,128,8,256]{3,1,2,0:T(8,128)(2,1)S(1)} %bitcast.10) | data formatting | bytes 1048576
  97.5 4.6 %collective-permute-done.2.pair_ref = bf16[2,256,128]{2,1,0:T(8,128)(2,1)S(1)} collective-permute-done((bf16[2,256,128]{2,1,0:T(8,128)(2,1)S(1)}, bf16[2,256,128]{2,1,0:T(8,128)(2,1)S(1)}, u32[]{:S(2)}, u32[]{:S(2)}) %collective-permute-start.2) | collective-permute-done | bytes 131104 | tf_op jit(solution)/shard_map/ppermute | solution.py:63
  102.1 0.9 shard_map.99
  103.0 1.1 %shard_map.101 = (f32[32,256]{1,0:T(8,128)}, f32[32,256]{1,0:T(8,128)}, f32[1024,128]{1,0:T(8,128)}) custom-call(bf16[32,48,128]{2,1,0:T(8,128)(2,1)S(1)} %all-to-all-done.5.in_ref), custom_call_target="tpu_custom_call" | custom-call | bytes 983040 | tf_op jit(solution)/shard_map/pallas_call | solution.py:46
  (8 shorter events, 0.0 us)
Async XLA Ops:
  0.6 1.3 %copy-start = (bf16[256,32]{0,1:T(8,128)(2,1)S(1)}, bf16[256,32]{0,1:T(8,128)(2,1)}, u32[]{:S(2)}) copy-start(bf16[256,32]{0,1:T(8,128)(2,1)} %param.6) | copy-start | bytes 49156
  0.6 1.3 %copy-start.1 = (bf16[256,32]{0,1:T(8,128)(2,1)S(1)}, bf16[256,32]{0,1:T(8,128)(2,1)}, u32[]{:S(2)}) copy-start(bf16[256,32]{0,1:T(8,128)(2,1)} %param.7) | copy-start | bytes 49156
  2.0 11.5 %copy-start.2 = (bf16[1024,128]{1,0:T(8,128)(2,1)S(1)}, bf16[1024,128]{1,0:T(8,128)(2,1)}, u32[]{:S(2)}) copy-start(bf16[1024,128]{1,0:T(8,128)(2,1)} %w_ref.1) | copy-start | bytes 786436
  40.6 12.3 %all-to-all-start.2 = ((bf16[4,256,128]{2,1,0:T(8,128)(2,1)}), bf16[4,256,128]{2,1,0:T(8,128)(2,1)S(1)}, u32[]{:S(2)}, u32[]{:S(2)}) async-start(bf16[4,256,128]{2,1,0:T(8,128)(2,1)} %get-tuple-element.34), calls=%async_computation.2 | async-start | bytes 524288 | tf_op jit(solution)/shard_map/all_to_all | solution.py:67
  46.2 6.8 %collective-permute-start = (bf16[1024,128]{1,0:T(8,128)(2,1)S(1)}, bf16[1024,128]{1,0:T(8,128)(2,1)S(1)}, u32[]{:S(2)}, u32[]{:S(2)}) collective-permute-start(bf16[1024,128]{1,0:T(8,128)(2,1)S(1)} %get-tuple-element.35.gout_ref), channel_id=1, source_target_pairs={{0,16},{16,0},{1,17},{17,1},{2,18},{18,2},{3,19},{19,3},{4,20},{20... | collective-permute-start | bytes 786440 | tf_op jit(solution)/shard_map/ppermute | solution.py:303
  66.6 18.3 %all-to-all-start.4 = ((bf16[16,48,128]{2,1,0:T(8,128)(2,1)}), bf16[16,48,128]{2,1,0:T(8,128)(2,1)S(1)}, u32[]{:S(2)}, u32[]{:S(2)}) async-start(bf16[16,48,128]{2,1,0:T(8,128)(2,1)} %get-tuple-element.38), calls=%async_computation.4 | async-start | bytes 393216 | tf_op jit(solution)/shard_map/all_to_all | solution.py:67
  73.2 6.8 %collective-permute-start.1 = (bf16[2,256,128]{2,1,0:T(8,128)(2,1)S(1)}, bf16[2,256,128]{2,1,0:T(8,128)(2,1)S(1)}, u32[]{:S(2)}, u32[]{:S(2)}) collective-permute-start(bf16[2,256,128]{2,1,0:T(8,128)(2,1)S(1)} %get-tuple-element.39), channel_id=1, source_target_pairs={{0,2},{1,3},{2,0},{3,1},{4,6},{5,7},{6,4},{7,5},{8,10},{9,11},{10,... | collective-permute-start | bytes 393224 | tf_op jit(solution)/shard_map/ppermute | solution.py:63
  85.7 17.3 %all-to-all-start.5 = ((bf16[32,48,128]{2,1,0:T(8,128)(2,1)}), bf16[32,48,128]{2,1,0:T(8,128)(2,1)S(1)}, u32[]{:S(2)}, u32[]{:S(2)}) async-start(bf16[32,48,128]{2,1,0:T(8,128)(2,1)} %get-tuple-element.45), calls=%async_computation.5 | async-start | bytes 786432 | tf_op jit(solution)/shard_map/all_to_all | solution.py:67
  92.8 9.3 %collective-permute-start.2 = (bf16[2,256,128]{2,1,0:T(8,128)(2,1)S(1)}, bf16[2,256,128]{2,1,0:T(8,128)(2,1)S(1)}, u32[]{:S(2)}, u32[]{:S(2)}) collective-permute-start(bf16[2,256,128]{2,1,0:T(8,128)(2,1)S(1)} %get-tuple-element.42), channel_id=1, source_target_pairs={{0,1},{1,0},{2,3},{3,2},{4,5},{5,4},{6,7},{7,6},{8,9},{9,8},{10,11... | collective-permute-start | bytes 393224 | tf_op jit(solution)/shard_map/ppermute | solution.py:63

commit v8 on v7

--- a/solution.py
+++ b/solution.py
@@ -206,7 +206,8 @@
     pair_ref[1] = got_ref[1]
 
 
-def update_kernel(own_ref, a_ref, pair_ref, out_ref):
+def update_kernel(own_ref, a_ref, pair_ref, after_ref, out_ref):
+    del after_ref
     me = place()
     for k, block in enumerate((own_ref[...], pair_ref[0], a_ref[...], pair_ref[1])):
         b = lax.bitwise_xor(me, k)
@@ -320,7 +321,6 @@
     tail, own, near, second = call(
         join_kernel, [shape((32, 48, 128), BF16), part, part, pair], tail, update, partner(first, 2)
     )
-    (update,) = call(update_kernel, [shape((RES * 128, Z), F32)], own, near, partner(second, 1))
     tail = exchange(tail, NEAR)
     gl, gr, gout = call(
         final_kernel,
@@ -328,6 +328,7 @@
         tail,
         scratch=[pltpu.VMEM((1056, 128), F32)],
     )
+    (update,) = call(update_kernel, [shape((RES * 128, Z), F32)], own, near, partner(second, 1), gl)
     return update.reshape(1, RES, 128, Z), msa.transpose(1, 0, 2)[None], gl.T, gr.T, gout
 
 

time: 105 us -> 105 us (level)
    ppermute x2, waiting for transfers between devices: 8.83 us -> 4.27 us  [partner(): return lax.ppermute(x, ROW, [(b, b ^ k) for b in range(G)])]
    all_to_all x3, waiting for transfers between devices: 4.89 us -> 9.24 us  [exchange(): return lax.all_to_all(x, axes, split_axis=0, concat_axis=0, tiled=True)]
where the time goes in v8:
time: 105 us
  blocking collectives  45.7 us (44%)
  starting transfers between devices  30.7 us (29%)
  waiting for transfers between devices  14.7 us (14%)
  Pallas kernels  11 us (10%)
  local copies, waits for them, and re-layouts  1.86 us (2%)
    all_to_all x3, blocking collectives, exchange(): return lax.all_to_all(x, axes, split_axis=0, concat_axis=0, tiled=True)  45.7 us
    all_to_all x3, starting transfers between devices, exchange(): return lax.all_to_all(x, axes, split_axis=0, concat_axis=0, tiled=True)  19.3 us
    pallas_call x10, Pallas kernels, call(): pl.pallas_call(kernel, out_shape=out, in_specs=[pl.BlockSpec(memory_space...  11 us
    all_to_all x3, waiting for transfers between devices, exchange(): return lax.all_to_all(x, axes, split_axis=0, concat_axis=0, tiled=True)  9.24 us
    ppermute x2, starting transfers between devices, partner(): return lax.ppermute(x, ROW, [(b, b ^ k) for b in range(G)])  5.85 us
    ppermute x1, starting transfers between devices, per_device(): other = lax.ppermute(gout, 'core', [(0, 1), (1, 0)])  5.61 us
    ppermute x2, waiting for transfers between devices, partner(): return lax.ppermute(x, ROW, [(b, b ^ k) for b in range(G)])  4.27 us
  transfers between devices with their start and end apart: 6, of which 4 were waited for; matrix products, arithmetic and copies ran while one was open for 1% of the time, Pallas kernels for 1%

profile of v8, /device:TPU:1, one launch (start us, length us, event | category | flops | bytes accessed | tf_op | source)
XLA Modules:
  0.0 104.7 jit_solution(10227087498403721602)
XLA Ops:
  0.7 1.3 %shard_map.92 = (bf16[4,512,128]{2,1,0:T(8,128)(2,1)S(1)}, bf16[8,128,256]{2,1,0:T(8,128)(2,1)S(1)}) custom-call(bf16[1024,256]{1,0:T(8,128)(2,1)} %bitcast.17, f32[1024,128]{1,0:T(8,128)} %bitcast.18), custom_call_target="tpu_custom_call" | custom-call | flops 2000000000 | bytes 2097152 | tf_op jit(solution)/shard_map/pallas_call | solution.py:46
  2.0 0.5 shard_map.93
  2.5 11.0 %all_to_all.30.row_ref = bf16[4,512,128]{2,1,0:T(8,128)(2,1)S(1)} all-to-all(bf16[4,512,128]{2,1,0:T(8,128)(2,1)S(1)} %get-tuple-element.29), channel_id=1, replica_groups=mesh['yh'=4,'x'=4,'core'=2,'zh'=4,'zl'=2,'yl'=2] {'zl','yl'}, dimensions={0} | all-to-all | bytes 1048576 | tf_op jit(solution)/shard_map/all_to_all | solution.py:67
  13.5 2.6 %shard_map.94 = (bf16[4,512,128]{2,1,0:T(8,128)(2,1)S(1)}, bf16[1024,1024]{1,0:T(8,128)(2,1)S(1)}, bf16[128,1024]{1,0:T(8,128)(2,1)S(1)}) custom-call(bf16[4,512,128]{2,1,0:T(8,128)(2,1)S(1)} %all_to_all.30.row_ref, bf16[256,128]{1,0:T(8,128)(2,1)S(1)} %get-tuple-element.30.right_ref, bf16[1024,128]{1,0:T(8,128)(2,1)S(1)} %copy-done.3), custom_call_target="tpu_custom_call" | custom-call | flops 536870912 | bytes 3735552 | tf_op jit(solution)/shard_map/pallas_call | solution.py:46
  16.1 22.2 %all_to_all.31.col_ref = bf16[4,512,128]{2,1,0:T(8,128)(2,1)S(1)} all-to-all(bf16[4,512,128]{2,1,0:T(8,128)(2,1)S(1)} %get-tuple-element.31), channel_id=1, replica_groups=mesh['yh'=4,'x'=4,'core'=2,'zh'=4,'zl'=2,'yl'=2] {'zh'}, dimensions={0} | all-to-all | bytes 1048576 | tf_op jit(solution)/shard_map/all_to_all | solution.py:67
  38.3 2.3 %shard_map.95 = (bf16[4,256,128]{2,1,0:T(8,128)(2,1)}, bf16[4,256,128]{2,1,0:T(8,128)(2,1)S(1)}, bf16[1024,128]{1,0:T(8,128)(2,1)S(1)}) custom-call(bf16[4,512,128]{2,1,0:T(8,128)(2,1)S(1)} %all_to_all.30.row_ref, bf16[4,512,128]{2,1,0:T(8,128)(2,1)S(1)} %all_to_all.31.col_ref, bf16[1024,1024]{1,0:T(8,128)(2,1)S(1)} %get-tuple-element.32.grads_ref, ...), custom_call_target="tpu_custom_call" | custom-call | flops 1073741824 | bytes 4194304 | tf_op jit(solution)/shard_map/pallas_call | solution.py:46
  40.6 5.6 %all-to-all-start.2 = ((bf16[4,256,128]{2,1,0:T(8,128)(2,1)}), bf16[4,256,128]{2,1,0:T(8,128)(2,1)S(1)}, u32[]{:S(2)}, u32[]{:S(2)}) async-start(bf16[4,256,128]{2,1,0:T(8,128)(2,1)} %get-tuple-element.34), calls=%async_computation.2 | async-start | bytes 524288 | tf_op jit(solution)/shard_map/all_to_all | solution.py:67
  46.2 5.6 %collective-permute-start = (bf16[1024,128]{1,0:T(8,128)(2,1)S(1)}, bf16[1024,128]{1,0:T(8,128)(2,1)S(1)}, u32[]{:S(2)}, u32[]{:S(2)}) collective-permute-start(bf16[1024,128]{1,0:T(8,128)(2,1)S(1)} %get-tuple-element.35.gout_ref), channel_id=1, source_target_pairs={{0,16},{16,0},{1,17},{17,1},{2,18},{18,2},{3,19},{19,3},{4,20},{20... | collective-permute-start | bytes 786440 | tf_op jit(solution)/shard_map/ppermute | solution.py:304
  51.8 1.1 %collective-permute-done.other_ref = bf16[1024,128]{1,0:T(8,128)(2,1)S(1)} collective-permute-done((bf16[1024,128]{1,0:T(8,128)(2,1)S(1)}, bf16[1024,128]{1,0:T(8,128)(2,1)S(1)}, u32[]{:S(2)}, u32[]{:S(2)}) %collective-permute-start) | collective-permute-done | bytes 262176 | tf_op jit(solution)/shard_map/ppermute | solution.py:304
  53.0 0.4 shard_map.96
  53.4 12.5 %all_to_all.32.in_ref = bf16[16,48,128]{2,1,0:T(8,128)(2,1)S(1)} all-to-all(bf16[16,48,128]{2,1,0:T(8,128)(2,1)S(1)} %get-tuple-element.36), channel_id=1, replica_groups=mesh['yh'=4,'x'=4,'core'=2,'zh'=4,'zl'=2,'yl'=2] {'x','zl','yl'}, dimensions={0} | all-to-all | bytes 393216 | tf_op jit(solution)/shard_map/all_to_all | solution.py:67
  65.9 0.7 shard_map.97
  66.6 6.6 %all-to-all-start.4 = ((bf16[16,48,128]{2,1,0:T(8,128)(2,1)}), bf16[16,48,128]{2,1,0:T(8,128)(2,1)S(1)}, u32[]{:S(2)}, u32[]{:S(2)}) async-start(bf16[16,48,128]{2,1,0:T(8,128)(2,1)} %get-tuple-element.38), calls=%async_computation.4 | async-start | bytes 393216 | tf_op jit(solution)/shard_map/all_to_all | solution.py:67
  73.2 2.6 %collective-permute-start.1 = (bf16[2,256,128]{2,1,0:T(8,128)(2,1)S(1)}, bf16[2,256,128]{2,1,0:T(8,128)(2,1)S(1)}, u32[]{:S(2)}, u32[]{:S(2)}) collective-permute-start(bf16[2,256,128]{2,1,0:T(8,128)(2,1)S(1)} %get-tuple-element.39), channel_id=1, source_target_pairs={{0,2},{1,3},{2,0},{3,1},{4,6},{5,7},{6,4},{7,5},{8,10},{9,11},{10,... | collective-permute-start | bytes 393224 | tf_op jit(solution)/shard_map/ppermute | solution.py:63
  75.7 4.3 %collective-permute-done.1.got_ref = bf16[2,256,128]{2,1,0:T(8,128)(2,1)S(1)} collective-permute-done((bf16[2,256,128]{2,1,0:T(8,128)(2,1)S(1)}, bf16[2,256,128]{2,1,0:T(8,128)(2,1)S(1)}, u32[]{:S(2)}, u32[]{:S(2)}) %collective-permute-start.1) | collective-permute-done | bytes 131104 | tf_op jit(solution)/shard_map/ppermute | solution.py:63
  80.0 4.9 %all-to-all-done.4.in_ref = bf16[16,48,128]{2,1,0:T(8,128)(2,1)S(1)} async-done(((bf16[16,48,128]{2,1,0:T(8,128)(2,1)}), bf16[16,48,128]{2,1,0:T(8,128)(2,1)S(1)}, u32[]{:S(2)}, u32[]{:S(2)}) %all-to-all-start.4) | async-done | bytes 196640 | tf_op jit(solution)/shard_map/all_to_all | solution.py:67
  84.9 0.8 shard_map.98
  85.7 7.2 %all-to-all-start.5 = ((bf16[32,48,128]{2,1,0:T(8,128)(2,1)}), bf16[32,48,128]{2,1,0:T(8,128)(2,1)S(1)}, u32[]{:S(2)}, u32[]{:S(2)}) async-start(bf16[32,48,128]{2,1,0:T(8,128)(2,1)} %get-tuple-element.43), calls=%async_computation.5 | async-start | bytes 786432 | tf_op jit(solution)/shard_map/all_to_all | solution.py:67
  92.8 3.3 %collective-permute-start.2 = (bf16[2,256,128]{2,1,0:T(8,128)(2,1)S(1)}, bf16[2,256,128]{2,1,0:T(8,128)(2,1)S(1)}, u32[]{:S(2)}, u32[]{:S(2)}) collective-permute-start(bf16[2,256,128]{2,1,0:T(8,128)(2,1)S(1)} %get-tuple-element.42), channel_id=1, source_target_pairs={{0,1},{1,0},{2,3},{3,2},{4,5},{5,4},{6,7},{7,6},{8,9},{9,8},{10,11... | collective-permute-start | bytes 393224 | tf_op jit(solution)/shard_map/ppermute | solution.py:63
  96.5 1.1 %copy.11 = bf16[1,128,8,256]{3,2,1,0:T(8,128)(2,1)} copy(bf16[1,128,8,256]{3,1,2,0:T(8,128)(2,1)S(1)} %bitcast.10) | data formatting | bytes 1048576
  97.5 4.4 %all-to-all-done.5.in_ref = bf16[32,48,128]{2,1,0:T(8,128)(2,1)S(1)} async-done(((bf16[32,48,128]{2,1,0:T(8,128)(2,1)}), bf16[32,48,128]{2,1,0:T(8,128)(2,1)S(1)}, u32[]{:S(2)}, u32[]{:S(2)}) %all-to-all-start.5) | async-done | bytes 393248 | tf_op jit(solution)/shard_map/all_to_all | solution.py:67
  101.9 1.1 %shard_map.99 = (f32[32,256]{1,0:T(8,128)}, f32[32,256]{1,0:T(8,128)}, f32[1024,128]{1,0:T(8,128)}) custom-call(bf16[32,48,128]{2,1,0:T(8,128)(2,1)S(1)} %all-to-all-done.5.in_ref), custom_call_target="tpu_custom_call" | custom-call | bytes 983040 | tf_op jit(solution)/shard_map/pallas_call | solution.py:46
  103.1 0.8 copy-done.2
  103.8 0.9 shard_map.100
  (10 shorter events, 0.3 us)
Async XLA Ops:
  0.6 1.3 %copy-start = (bf16[256,32]{0,1:T(8,128)(2,1)S(1)}, bf16[256,32]{0,1:T(8,128)(2,1)}, u32[]{:S(2)}) copy-start(bf16[256,32]{0,1:T(8,128)(2,1)} %param.6) | copy-start | bytes 49156
  0.6 1.3 %copy-start.1 = (bf16[256,32]{0,1:T(8,128)(2,1)S(1)}, bf16[256,32]{0,1:T(8,128)(2,1)}, u32[]{:S(2)}) copy-start(bf16[256,32]{0,1:T(8,128)(2,1)} %param.7) | copy-start | bytes 49156
  2.0 11.5 %copy-start.3 = (bf16[1024,128]{1,0:T(8,128)(2,1)S(1)}, bf16[1024,128]{1,0:T(8,128)(2,1)}, u32[]{:S(2)}) copy-start(bf16[1024,128]{1,0:T(8,128)(2,1)} %w_ref.1) | copy-start | bytes 786436
  40.6 12.3 %all-to-all-start.2 = ((bf16[4,256,128]{2,1,0:T(8,128)(2,1)}), bf16[4,256,128]{2,1,0:T(8,128)(2,1)S(1)}, u32[]{:S(2)}, u32[]{:S(2)}) async-start(bf16[4,256,128]{2,1,0:T(8,128)(2,1)} %get-tuple-element.34), calls=%async_computation.2 | async-start | bytes 524288 | tf_op jit(solution)/shard_map/all_to_all | solution.py:67
  46.2 6.8 %collective-permute-start = (bf16[1024,128]{1,0:T(8,128)(2,1)S(1)}, bf16[1024,128]{1,0:T(8,128)(2,1)S(1)}, u32[]{:S(2)}, u32[]{:S(2)}) collective-permute-start(bf16[1024,128]{1,0:T(8,128)(2,1)S(1)} %get-tuple-element.35.gout_ref), channel_id=1, source_target_pairs={{0,16},{16,0},{1,17},{17,1},{2,18},{18,2},{3,19},{19,3},{4,20},{20... | collective-permute-start | bytes 786440 | tf_op jit(solution)/shard_map/ppermute | solution.py:304
  66.6 18.3 %all-to-all-start.4 = ((bf16[16,48,128]{2,1,0:T(8,128)(2,1)}), bf16[16,48,128]{2,1,0:T(8,128)(2,1)S(1)}, u32[]{:S(2)}, u32[]{:S(2)}) async-start(bf16[16,48,128]{2,1,0:T(8,128)(2,1)} %get-tuple-element.38), calls=%async_computation.4 | async-start | bytes 393216 | tf_op jit(solution)/shard_map/all_to_all | solution.py:67
  73.2 6.8 %collective-permute-start.1 = (bf16[2,256,128]{2,1,0:T(8,128)(2,1)S(1)}, bf16[2,256,128]{2,1,0:T(8,128)(2,1)S(1)}, u32[]{:S(2)}, u32[]{:S(2)}) collective-permute-start(bf16[2,256,128]{2,1,0:T(8,128)(2,1)S(1)} %get-tuple-element.39), channel_id=1, source_target_pairs={{0,2},{1,3},{2,0},{3,1},{4,6},{5,7},{6,4},{7,5},{8,10},{9,11},{10,... | collective-permute-start | bytes 393224 | tf_op jit(solution)/shard_map/ppermute | solution.py:63
  85.7 16.2 %all-to-all-start.5 = ((bf16[32,48,128]{2,1,0:T(8,128)(2,1)}), bf16[32,48,128]{2,1,0:T(8,128)(2,1)S(1)}, u32[]{:S(2)}, u32[]{:S(2)}) async-start(bf16[32,48,128]{2,1,0:T(8,128)(2,1)} %get-tuple-element.43), calls=%async_computation.5 | async-start | bytes 786432 | tf_op jit(solution)/shard_map/all_to_all | solution.py:67
  92.8 10.2 %collective-permute-start.2 = (bf16[2,256,128]{2,1,0:T(8,128)(2,1)S(1)}, bf16[2,256,128]{2,1,0:T(8,128)(2,1)S(1)}, u32[]{:S(2)}, u32[]{:S(2)}) collective-permute-start(bf16[2,256,128]{2,1,0:T(8,128)(2,1)S(1)} %get-tuple-element.42), channel_id=1, source_target_pairs={{0,1},{1,0},{2,3},{3,2},{4,5},{5,4},{6,7},{7,6},{8,9},{9,8},{10,11... | collective-permute-start | bytes 393224 | tf_op jit(solution)/shard_map/ppermute | solution.py:63
  103.0 0.8 copy-start.2
